TPU v7x, 32 devices: a whole 2x2x4 slice. The times are simulated.
32 devices in a mesh: row: 4 (over y, x), col: 8 (over z, core).
Axes of the slice: x: 2, y: 2, z: 4, core: 2. Of those that a mesh axis runs over, the one named last changes fastest.
Arguments:
- upper_blocks: bfloat16 [4, 8, 63, 128, 128], P('row', 'col'), may hold values from -1.5 to 1.5
- block_targets: int32 [4, 8, 63], P('row', 'col'), may hold values from 0 to 7, as said below
- product_plan: int32 [4, 8, 2, 128, 3], P('row', 'col'), may hold values from 0 to 125, as said below
- live_counts: int32 [4, 8, 2], P('row', 'col'), may hold values from 24 to 128, as said below
Outputs:
- result_blocks: bfloat16 [4, 8, 32, 128, 128], P('row', 'col')
Inputs may be any that keep to these rules, and one draw needn't show every extreme that they name: `block_targets`: A device's stored blocks never target its own column; within one grid row, the k-th stored block of every device targets the same number of columns onward, and at most 9 of a device's blocks target one column, reached in every draw. `product_plan`: columns 0 and 1 name panel blocks below 126, column 2 a result block below 32. In section 1, all 128 slots of a device together name exactly 24 distinct left blocks and exactly 24 distinct right blocks. `live_counts`: in each section some device has all 128 slots live.
All inputs are finite; a program needn't handle non-finite values.
Results may differ from a plain program's by a relative error of at most 0.008.
Values may be sent and summed in bfloat16 or wider, within the bound.
No kernel may reach another device: no remote copies, remote signals or barrier semaphores. Data moves between devices by JAX's collectives and lax.ppermute only.
A program may use at most 64 MiB of HBM per device.

v0:
```python
import math

import jax
import jax.numpy as jnp
from jax import lax
from jax.sharding import PartitionSpec as P

OUTSLOTS = 32


def shifted(value, axis, steps):
    count = lax.axis_size(axis)
    pairs = [(source, (source + steps) % count) for source in range(count)]
    return lax.ppermute(value, axis, pairs)


def select_blocks(panel, indices):
    slots, block, _ = panel.shape
    onehot = (indices[:, None] == jnp.arange(slots, dtype=jnp.int32)[None, :]).astype(jnp.bfloat16)
    flat = panel.reshape(slots, block * block)
    picked = jnp.dot(onehot, flat, preferred_element_type=jnp.float32).astype(jnp.bfloat16)
    return picked.reshape(indices.shape[0], block, block)


def accumulate(total, left_panel, right_panel, left_index, right_index, out_index, count):
    length = left_index.shape[0]
    group = math.gcd(length, 32)
    result_count, block, _ = total.shape
    slot_ids = jnp.arange(result_count, dtype=jnp.int32)

    def advance(counter, running):
        start = counter * group
        left_pick = lax.dynamic_slice_in_dim(left_index, start, group)
        right_pick = lax.dynamic_slice_in_dim(right_index, start, group)
        out_pick = lax.dynamic_slice_in_dim(out_index, start, group)
        left_rows = select_blocks(left_panel, left_pick)
        right_rows = select_blocks(right_panel, right_pick)
        terms = jnp.einsum(
            "pij,pjk->pik", left_rows, right_rows, preferred_element_type=jnp.float32
        )
        terms = terms.reshape(group, block * block)
        alive = start + jnp.arange(group, dtype=jnp.int32) < count
        weights = ((out_pick[:, None] == slot_ids[None, :]) & alive[:, None]).astype(jnp.bfloat16)
        high_part = terms.astype(jnp.bfloat16)
        remainder = terms - high_part.astype(jnp.float32)
        middle_part = remainder.astype(jnp.bfloat16)
        low_part = (remainder - middle_part.astype(jnp.float32)).astype(jnp.bfloat16)
        added = jnp.einsum("po,pn->on", weights, high_part, preferred_element_type=jnp.float32)
        added = added + jnp.einsum(
            "po,pn->on", weights, middle_part, preferred_element_type=jnp.float32
        )
        added = added + jnp.einsum(
            "po,pn->on", weights, low_part, preferred_element_type=jnp.float32
        )
        return running + added.reshape(result_count, block, block)

    return lax.fori_loop(0, length // group, advance, total)


def body(upper_blocks, block_targets, product_plan, live_counts):
    stored_blocks = upper_blocks[0, 0]
    targets = block_targets[0, 0]
    plan = product_plan[0, 0]
    counts = live_counts[0, 0]
    stored, block, _ = stored_blocks.shape
    col_count = lax.axis_size("col")
    my_col = lax.axis_index("col")
    capacity = (stored + col_count - 2) // (col_count - 1)
    slot_ids = jnp.arange(stored, dtype=jnp.int32)
    earlier = (targets[None, :] == targets[:, None]) & (slot_ids[None, :] < slot_ids[:, None])
    ranks = jnp.sum(earlier.astype(jnp.int32), axis=1)
    bucket_ids = targets * capacity + ranks
    onehot = (
        bucket_ids[:, None] == jnp.arange(col_count * capacity, dtype=jnp.int32)[None, :]
    ).astype(jnp.bfloat16)
    flipped = jnp.swapaxes(stored_blocks, 1, 2)
    buckets = jnp.einsum("kn,kij->nij", onehot, flipped, preferred_element_type=jnp.float32).astype(
        jnp.bfloat16
    )
    buckets = buckets.reshape(col_count, capacity, block, block)
    received = lax.all_to_all(buckets, "col", split_axis=0, concat_axis=0, tiled=True)
    offsets = (targets - my_col) % col_count
    sources = (my_col - offsets) % col_count
    lower_blocks = select_blocks(
        received.reshape(col_count * capacity, block, block), sources * capacity + ranks
    )
    panel = jnp.concatenate([stored_blocks, lower_blocks], axis=0)
    total = jnp.zeros((OUTSLOTS, block, block), jnp.float32)
    total = accumulate(total, panel, panel, plan[0, :, 0], plan[0, :, 1], plan[0, :, 2], counts[0])
    left_source = shifted(panel, "col", -1)
    right_source = shifted(panel, "row", -1)
    left_index = plan[1, :, 0]
    right_index = plan[1, :, 1]
    total = accumulate(
        total, left_source, right_source, left_index, right_index, plan[1, :, 2], counts[1]
    )
    return total.astype(jnp.bfloat16)[None, None]


def solution(mesh):
    placed = (
        P("row", "col", None, None, None),
        P("row", "col", None),
        P("row", "col", None, None, None),
        P("row", "col", None),
    )
    return jax.shard_map(
        body,
        mesh=mesh,
        in_specs=placed,
        out_specs=P("row", "col", None, None, None),
        check_vma=False,
    )
```

profile of v0, /device:TPU:31, one launch (start us, length us, event | category | flops | bytes accessed | tf_op | source)
XLA Modules:
  0.0 265.6 jit_solution(5910012108457584779)
XLA Ops:
  0.0 3.3 %copy.8 = bf16[63,128,128]{2,0,1:T(8,128)(2,1)S(1)} copy(bf16[63,128,128]{1,2,0:T(8,128)(2,1)} %bitcast.191) | data formatting | bytes 4128768 | tf_op jit(solution)/shard_map/transpose | solution.py:76
  6.4 5.5 %all-to-all-start = ((bf16[8,9,128,128]{3,2,1,0:T(8,128)(2,1)}), bf16[8,9,128,128]{3,2,1,0:T(8,128)(2,1)}, u32[]{:S(2)}, u32[]{:S(2)}) async-start(bf16[8,9,128,128]{3,2,1,0:T(8,128)(2,1)} %bitcast.188), calls=%async_computation | async-start | bytes 4718592 | tf_op jit(solution)/shard_map/all_to_all | solution.py:81
  12.6 51.5 %all-to-all-done = bf16[8,9,128,128]{3,2,1,0:T(8,128)(2,1)} async-done(((bf16[8,9,128,128]{3,2,1,0:T(8,128)(2,1)}), bf16[8,9,128,128]{3,2,1,0:T(8,128)(2,1)}, u32[]{:S(2)}, u32[]{:S(2)}) %all-to-all-start) | async-done | bytes 2359328 | tf_op jit(solution)/shard_map/all_to_all | solution.py:81
  64.1 3.6 %convolution_convert_fusion.4 = bf16[63,16384]{1,0:T(8,128)(2,1)S(1)} fusion(bf16[9,8,128,128]{3,2,1,0:T(8,128)(2,1)} %bitcast.42, s32[63]{0:T(128)S(1)} %get-tuple-element.380), kind=kOutput, calls=%fused_computation.54 | convolution fusion | flops 149672384 | bytes 4423932 | tf_op jit(solution)/shard_map/dot_general | solution.py:21
  72.9 89.5 %while.29 = (s32[]{:T(128)}, f32[32,128,128]{2,1,0:T(8,128)S(1)}, s32[128]{0:T(128)S(1)}, s32[]{:T(128)}, s32[128]{0:T(128)S(1)}, /*index=5*/bf16[126,128,128]{2...) while((s32[]{:T(128)}, f32[32,128,128]{2,1,0:T(8,128)S(1)}, ...), condition=%wide.region_2.3_spmd.clone, body=%wide.region_1.2_spmd.clone.sunk | while | flops 508049344 | bytes 79496928 | solution.py:57
  72.9 2.5 pad.12
  75.4 5.6 %copy.79 = bf16[16,8,128,128]{3,1,2,0:T(8,128)(2,1)} copy(bf16[16,8,128,128]{3,2,1,0:T(8,128)(2,1)S(1)} %bitcast.181) | data formatting | bytes 8388608 | tf_op jit(solution)/shard_map/while
  81.0 3.1 %fusion.111 = bf16[4,8,128,128]{3,1,2,0:T(8,128)(2,1)S(1)} fusion(bf16[126,16384]{1,0:T(8,128)(2,1)} %bitcast.171, s32[32]{0:T(128)S(1)} %dynamic_slice.57), kind=kOutput, calls=%fused_computation.39.clone.1 | convolution fusion | flops 132648896 | bytes 5177472 | tf_op jit(solution)/shard_map/while/body/eval_jaxpr/dot_general | solution.py:21
  95.3 2.5 pad.12
  97.8 5.6 %copy.79 = bf16[16,8,128,128]{3,1,2,0:T(8,128)(2,1)} copy(bf16[16,8,128,128]{3,2,1,0:T(8,128)(2,1)S(1)} %bitcast.181) | data formatting | bytes 8388608 | tf_op jit(solution)/shard_map/while
  103.4 3.1 %fusion.111 = bf16[4,8,128,128]{3,1,2,0:T(8,128)(2,1)S(1)} fusion(bf16[126,16384]{1,0:T(8,128)(2,1)} %bitcast.171, s32[32]{0:T(128)S(1)} %dynamic_slice.57), kind=kOutput, calls=%fused_computation.39.clone.1 | convolution fusion | flops 132648896 | bytes 5177472 | tf_op jit(solution)/shard_map/while/body/eval_jaxpr/dot_general | solution.py:21
  120.2 5.6 %copy.79 = bf16[16,8,128,128]{3,1,2,0:T(8,128)(2,1)} copy(bf16[16,8,128,128]{3,2,1,0:T(8,128)(2,1)S(1)} %bitcast.181) | data formatting | bytes 8388608 | tf_op jit(solution)/shard_map/while
  125.8 3.1 %fusion.111 = bf16[4,8,128,128]{3,1,2,0:T(8,128)(2,1)S(1)} fusion(bf16[126,16384]{1,0:T(8,128)(2,1)} %bitcast.171, s32[32]{0:T(128)S(1)} %dynamic_slice.57), kind=kOutput, calls=%fused_computation.39.clone.1 | convolution fusion | flops 132648896 | bytes 5177472 | tf_op jit(solution)/shard_map/while/body/eval_jaxpr/dot_general | solution.py:21
  142.5 5.6 %copy.79 = bf16[16,8,128,128]{3,1,2,0:T(8,128)(2,1)} copy(bf16[16,8,128,128]{3,2,1,0:T(8,128)(2,1)S(1)} %bitcast.181) | data formatting | bytes 8388608 | tf_op jit(solution)/shard_map/while
  148.2 3.1 %fusion.111 = bf16[4,8,128,128]{3,1,2,0:T(8,128)(2,1)S(1)} fusion(bf16[126,16384]{1,0:T(8,128)(2,1)} %bitcast.171, s32[32]{0:T(128)S(1)} %dynamic_slice.57), kind=kOutput, calls=%fused_computation.39.clone.1 | convolution fusion | flops 132648896 | bytes 5177472 | tf_op jit(solution)/shard_map/while/body/eval_jaxpr/dot_general | solution.py:21
  164.6 99.8 %while.28 = (s32[]{:T(128)}, f32[32,128,128]{2,1,0:T(8,128)S(1)}, s32[128]{0:T(128)S(1)}, s32[]{:T(128)}, s32[128]{0:T(128)S(1)}, /*index=5*/bf16[126,128,128]{2...) while((s32[]{:T(128)}, f32[32,128,128]{2,1,0:T(8,128)S(1)}, ...), condition=%wide.region_4.5_spmd.clone, body=%wide.region_3.4_spmd.clone.sunk | while | flops 507525056 | bytes 79431368 | solution.py:57
  167.1 5.6 %copy.71 = bf16[16,8,128,128]{3,1,2,0:T(8,128)(2,1)} copy(bf16[16,8,128,128]{3,2,1,0:T(8,128)(2,1)S(1)} %bitcast.183) | data formatting | bytes 8388608 | tf_op jit(solution)/shard_map/while
  172.8 2.9 %fusion.98 = bf16[4,8,128,128]{3,1,2,0:T(8,128)(2,1)S(1)} fusion(bf16[126,16384]{1,0:T(8,128)(2,1)} %bitcast.179, s32[32]{0:T(128)S(1)} %dynamic_slice.54), kind=kOutput, calls=%fused_computation.13.clone.1 | convolution fusion | flops 132648896 | bytes 5177472 | tf_op jit(solution)/shard_map/while/body/eval_jaxpr/dot_general | solution.py:21
  175.9 2.5 pad.11
  178.4 3.5 %copy.73 = bf16[16,8,128,128]{3,1,2,0:T(8,128)(2,1)S(1)} copy(bf16[16,8,128,128]{3,2,1,0:T(8,128)(2,1)S(1)} %bitcast.182) | data formatting | bytes 8388608 | tf_op jit(solution)/shard_map/while
  192.1 5.6 %copy.71 = bf16[16,8,128,128]{3,1,2,0:T(8,128)(2,1)} copy(bf16[16,8,128,128]{3,2,1,0:T(8,128)(2,1)S(1)} %bitcast.183) | data formatting | bytes 8388608 | tf_op jit(solution)/shard_map/while
  197.7 2.9 %fusion.98 = bf16[4,8,128,128]{3,1,2,0:T(8,128)(2,1)S(1)} fusion(bf16[126,16384]{1,0:T(8,128)(2,1)} %bitcast.179, s32[32]{0:T(128)S(1)} %dynamic_slice.54), kind=kOutput, calls=%fused_computation.13.clone.1 | convolution fusion | flops 132648896 | bytes 5177472 | tf_op jit(solution)/shard_map/while/body/eval_jaxpr/dot_general | solution.py:21
  200.9 2.5 pad.11
  203.4 3.5 %copy.73 = bf16[16,8,128,128]{3,1,2,0:T(8,128)(2,1)S(1)} copy(bf16[16,8,128,128]{3,2,1,0:T(8,128)(2,1)S(1)} %bitcast.182) | data formatting | bytes 8388608 | tf_op jit(solution)/shard_map/while
  217.0 5.6 %copy.71 = bf16[16,8,128,128]{3,1,2,0:T(8,128)(2,1)} copy(bf16[16,8,128,128]{3,2,1,0:T(8,128)(2,1)S(1)} %bitcast.183) | data formatting | bytes 8388608 | tf_op jit(solution)/shard_map/while
  222.7 2.9 %fusion.98 = bf16[4,8,128,128]{3,1,2,0:T(8,128)(2,1)S(1)} fusion(bf16[126,16384]{1,0:T(8,128)(2,1)} %bitcast.179, s32[32]{0:T(128)S(1)} %dynamic_slice.54), kind=kOutput, calls=%fused_computation.13.clone.1 | convolution fusion | flops 132648896 | bytes 5177472 | tf_op jit(solution)/shard_map/while/body/eval_jaxpr/dot_general | solution.py:21
  225.8 2.5 pad.11
  228.3 3.5 %copy.73 = bf16[16,8,128,128]{3,1,2,0:T(8,128)(2,1)S(1)} copy(bf16[16,8,128,128]{3,2,1,0:T(8,128)(2,1)S(1)} %bitcast.182) | data formatting | bytes 8388608 | tf_op jit(solution)/shard_map/while
  242.0 5.6 %copy.71 = bf16[16,8,128,128]{3,1,2,0:T(8,128)(2,1)} copy(bf16[16,8,128,128]{3,2,1,0:T(8,128)(2,1)S(1)} %bitcast.183) | data formatting | bytes 8388608 | tf_op jit(solution)/shard_map/while
  247.6 2.9 %fusion.98 = bf16[4,8,128,128]{3,1,2,0:T(8,128)(2,1)S(1)} fusion(bf16[126,16384]{1,0:T(8,128)(2,1)} %bitcast.179, s32[32]{0:T(128)S(1)} %dynamic_slice.54), kind=kOutput, calls=%fused_computation.13.clone.1 | convolution fusion | flops 132648896 | bytes 5177472 | tf_op jit(solution)/shard_map/while/body/eval_jaxpr/dot_general | solution.py:21
  250.8 2.5 pad.11
  253.2 3.5 %copy.73 = bf16[16,8,128,128]{3,1,2,0:T(8,128)(2,1)S(1)} copy(bf16[16,8,128,128]{3,2,1,0:T(8,128)(2,1)S(1)} %bitcast.182) | data formatting | bytes 8388608 | tf_op jit(solution)/shard_map/while
  (141 shorter events, 103.3 us)
Async XLA Ops:
  0.0 3.3 %copy-start.4 = (s32[1,1,63]{2,1,0:T(1,128)S(1)}, s32[1,1,63]{2,1,0:T(1,128)}, u32[]{:S(2)}) copy-start(s32[1,1,63]{2,1,0:T(1,128)} %param.9) | copy-start | bytes 760
  6.4 5.6 %copy-start.3 = (s32[1,1,2]{2,1,0:T(1,128)S(1)}, s32[1,1,2]{2,1,0:T(1,128)}, u32[]{:S(2)}) copy-start(s32[1,1,2]{2,1,0:T(1,128)} %param.11) | copy-start | bytes 28
  6.4 6.1 %copy-start.2 = (s32[1,1,2,128,3]{3,2,4,1,0:T(2,128)S(1)}, s32[1,1,2,128,3]{3,2,4,1,0:T(2,128)}, u32[]{:S(2)}) copy-start(s32[1,1,2,128,3]{3,2,4,1,0:T(2,128)} %param.10) | copy-start | bytes 9220
  6.4 57.7 %all-to-all-start = ((bf16[8,9,128,128]{3,2,1,0:T(8,128)(2,1)}), bf16[8,9,128,128]{3,2,1,0:T(8,128)(2,1)}, u32[]{:S(2)}, u32[]{:S(2)}) async-start(bf16[8,9,128,128]{3,2,1,0:T(8,128)(2,1)} %bitcast.188), calls=%async_computation | async-start | bytes 4718592 | tf_op jit(solution)/shard_map/all_to_all | solution.py:81
  68.3 1.6 copy-start.1
  72.2 90.3 %collective-permute-start = (bf16[126,128,128]{2,1,0:T(8,128)(2,1)}, bf16[126,128,128]{2,1,0:T(8,128)(2,1)}, u32[]{:S(2)}, u32[]{:S(2)}) collective-permute-start(bf16[126,128,128]{2,1,0:T(8,128)(2,1)} %pad_maximum_fusion), channel_id=1, source_target_pairs={{0,7},{1,0},{2,1},{3,2},{4,3},{5,4},{6,5},{7,6},{8,15},{9,8},{10,9... | collective-permute-start | bytes 12386312 | tf_op jit(solution)/shard_map/ppermute | solution.py:14
  72.6 92.0 %collective-permute-start.1 = (bf16[126,128,128]{2,1,0:T(8,128)(2,1)}, bf16[126,128,128]{2,1,0:T(8,128)(2,1)}, u32[]{:S(2)}, u32[]{:S(2)}) collective-permute-start(bf16[126,128,128]{2,1,0:T(8,128)(2,1)} %pad_maximum_fusion), channel_id=1, source_target_pairs={{0,24},{8,0},{16,8},{24,16},{1,25},{9,1},{17,9},{25,17},{2,26},{10... | collective-permute-start | bytes 12386312 | tf_op jit(solution)/shard_map/ppermute | solution.py:14
  81.0 3.4 %copy-start = (bf16[16,8,128,128]{3,1,2,0:T(8,128)(2,1)S(1)}, bf16[16,8,128,128]{3,1,2,0:T(8,128)(2,1)}, u32[]{:S(2)}) copy-start(bf16[16,8,128,128]{3,1,2,0:T(8,128)(2,1)} %copy.79) | copy-start | bytes 12582916 | tf_op jit(solution)/shard_map/while
  103.4 3.4 %copy-start = (bf16[16,8,128,128]{3,1,2,0:T(8,128)(2,1)S(1)}, bf16[16,8,128,128]{3,1,2,0:T(8,128)(2,1)}, u32[]{:S(2)}) copy-start(bf16[16,8,128,128]{3,1,2,0:T(8,128)(2,1)} %copy.79) | copy-start | bytes 12582916 | tf_op jit(solution)/shard_map/while
  125.8 3.4 %copy-start = (bf16[16,8,128,128]{3,1,2,0:T(8,128)(2,1)S(1)}, bf16[16,8,128,128]{3,1,2,0:T(8,128)(2,1)}, u32[]{:S(2)}) copy-start(bf16[16,8,128,128]{3,1,2,0:T(8,128)(2,1)} %copy.79) | copy-start | bytes 12582916 | tf_op jit(solution)/shard_map/while
  148.2 3.4 %copy-start = (bf16[16,8,128,128]{3,1,2,0:T(8,128)(2,1)S(1)}, bf16[16,8,128,128]{3,1,2,0:T(8,128)(2,1)}, u32[]{:S(2)}) copy-start(bf16[16,8,128,128]{3,1,2,0:T(8,128)(2,1)} %copy.79) | copy-start | bytes 12582916 | tf_op jit(solution)/shard_map/while
where the time goes:
time: 271 us; the launch traced here: 266 us
  local copies, waits for them, and re-layouts  111 us (41%)
  matrix products  74.1 us (27%)
  waiting for transfers between devices  53.7 us (20%)
  other arithmetic  19.8 us (7%)
  starting transfers between devices  6.24 us (2%)
    while x56, local copies, waits for them, and re-layouts  101 us
    all_to_all x1, waiting for transfers between devices, body(): lax.all_to_all(buckets, 'col', split_axis=0, concat_axis=0, tiled=True)  51.5 us
    dot_general x17, matrix products, select_blocks(): jnp.dot(onehot, flat, preferred_element_type=jnp.float32)  33.2 us
    dot_general x8, matrix products, advance(): jnp.einsum('po,pn->on', weights, middle_part, preferred_element_type=jnp....  12.3 us
    dot_general x8, matrix products, advance(): jnp.einsum('po,pn->on', weights, low_part, preferred_element_type=jnp.flo...  12.2 us
    dot_general x8, matrix products, advance(): jnp.einsum('po,pn->on', weights, high_part, preferred_element_type=jnp.fl...  11.9 us
    add x8, other arithmetic, advance(): return running + added.reshape(result_count, block, block)  11.2 us
    all_to_all x1, starting transfers between devices, body(): lax.all_to_all(buckets, 'col', split_axis=0, concat_axis=0, tiled=True)  5.54 us
  transfers between devices with their start and end apart: 3, of which 2 were waited for; matrix products, arithmetic and copies ran while one was open for 34% of the time, Pallas kernels for 0%

commit v1 on v0

v1 whole, which is shorter than its diff:
```python
import functools

import jax
import jax.numpy as jnp
from jax import lax
from jax.experimental import pallas as pl
from jax.experimental.pallas import tpu as pltpu
from jax.sharding import PartitionSpec as P

OUTSLOTS = 32
USED = 24
UNROLL = 4
MIB = 1 << 20

SMEM = pl.BlockSpec(memory_space=pltpu.SMEM)
VMEM = pl.BlockSpec(memory_space=pltpu.VMEM)
HBM = pl.BlockSpec(memory_space=pltpu.HBM)


def i32(*shape):
    return jax.ShapeDtypeStruct(shape, jnp.int32)


def params(mib):
    return pltpu.CompilerParams(vmem_limit_bytes=mib * MIB)


def moved(value, axis, steps):
    count = lax.axis_size(axis)
    return lax.ppermute(value, axis, [(s, (s + steps) % count) for s in range(count)])


def after(value, *needed):
    return lax.optimization_barrier((value, *needed))[0]


class Layout:
    def __init__(self, stored, cols):
        self.stored = stored
        self.cols = cols
        self.cap = (stored + cols - 2) // (cols - 1)
        others = list(range(2, cols))
        half = cols // 2
        others.sort(key=lambda d: (half - abs(d - half), d))
        pieces = min(6, len(others))
        cuts = [len(others) * i // pieces for i in range(pieces + 1)]
        self.stages = [others[a:b] for a, b in zip(cuts, cuts[1:])] + [[1]]
        self.base = [0] * cols
        self.start = []
        at = 0
        for stage in self.stages:
            self.start.append(at)
            for d in stage:
                self.base[d] = at
                at += self.cap
        self.total = at
        self.start.append(at)

    def size(self, s):
        return self.start[s + 1] - self.start[s]


def sort_kernel(lay, tgt, col, stored_ref, out, pos, inv, buf, cnt, sem):
    me = col[0]
    for d in range(lay.cols):
        cnt[d] = lay.base[d]

    def place(k, carry):
        d = tgt[k] - me
        d = jnp.where(d < 0, d + lay.cols, d)
        q = cnt[d]
        cnt[d] = q + 1
        pos[k] = q
        inv[q] = k
        return carry

    lax.fori_loop(0, lay.stored, place, 0)
    n = lay.size(0)

    def fetch(j, carry):
        pltpu.make_async_copy(stored_ref.at[inv[j]], buf.at[j], sem).start()
        return carry

    lax.fori_loop(0, n, fetch, 0)
    pltpu.make_async_copy(buf, buf, sem).wait()

    def flip(j, carry):
        out[j] = buf[j].T
        return carry

    lax.fori_loop(0, n, flip, 0)


def first_stage(lay, targets, col, stored):
    block = stored.shape[-1]
    n = lay.size(0)
    return pl.pallas_call(
        functools.partial(sort_kernel, lay),
        out_shape=(jax.ShapeDtypeStruct((n, block, block), stored.dtype), i32(lay.stored), i32(lay.total)),
        in_specs=[SMEM, SMEM, HBM],
        out_specs=(VMEM, SMEM, SMEM),
        scratch_shapes=[
            pltpu.VMEM((n, block, block), stored.dtype),
            pltpu.SMEM((lay.cols,), jnp.int32),
            pltpu.SemaphoreType.DMA,
        ],
        compiler_params=params(8),
        name="sort_first",
    )(targets, col, stored)


def rest_kernel(lay, inv, stored_ref, *outs):
    for s in range(1, len(lay.stages)):

        def flip(j, carry, s=s):
            outs[s - 1][j] = stored_ref[inv[lay.start[s] + j]].T
            return carry

        lax.fori_loop(0, lay.size(s), flip, 0)


def rest_stages(lay, inv, stored):
    block = stored.shape[-1]
    shapes = tuple(
        jax.ShapeDtypeStruct((lay.size(s), block, block), stored.dtype) for s in range(1, len(lay.stages))
    )
    return pl.pallas_call(
        functools.partial(rest_kernel, lay),
        out_shape=shapes,
        in_specs=[SMEM, VMEM],
        out_specs=(VMEM,) * len(shapes),
        compiler_params=params(12),
        name="flip_rest",
    )(inv, stored)


def wanted_kernel(prods, plan, reqs_l, reqs_r, slots_l, slots_r, seen):
    for side, (reqs, slots) in enumerate(((reqs_l, slots_l), (reqs_r, slots_r))):

        def clear(i, carry):
            seen[i] = -1
            return carry

        lax.fori_loop(0, seen.shape[0], clear, 0)

        def clear_request(i, carry, reqs=reqs):
            reqs[i] = 0
            return carry

        lax.fori_loop(0, USED, clear_request, 0)

        def step(p, n, side=side, reqs=reqs, slots=slots):
            which = plan[side * prods + p]
            known = seen[which]
            fresh = known < 0
            slot = jnp.where(fresh, n, known)
            seen[which] = slot
            reqs[slot] = which
            slots[p] = slot
            return jnp.where(fresh, n + 1, n)

        lax.fori_loop(0, prods, step, 0)


def wanted(panel_size, plan_flat, prods):
    return pl.pallas_call(
        functools.partial(wanted_kernel, prods),
        out_shape=(i32(USED), i32(USED), i32(prods), i32(prods)),
        in_specs=[SMEM],
        out_specs=(SMEM,) * 4,
        scratch_shapes=[pltpu.SMEM((panel_size,), jnp.int32)],
        name="wanted",
    )(plan_flat)


def pick_kernel(lay, stages, req, pos, stored_ref, *rest):
    parts, out = rest[: len(stages)], rest[len(stages)]

    def step(n, carry):
        which = req[n]
        lower = which >= lay.stored
        q = pos[jnp.where(lower, which - lay.stored, 0)]

        @pl.when(jnp.logical_not(lower))
        def _():
            out[n] = stored_ref[which]

        for s, part in zip(stages, parts):

            @pl.when(lower & (q >= lay.start[s]) & (q < lay.start[s + 1]))
            def _(s=s, part=part):
                out[n] = part[q - lay.start[s]]

        return carry

    lax.fori_loop(0, USED, step, 0)


def pick(lay, stages, req, pos, stored, parts, name):
    block = stored.shape[-1]
    return pl.pallas_call(
        functools.partial(pick_kernel, lay, stages),
        out_shape=jax.ShapeDtypeStruct((USED, block, block), stored.dtype),
        in_specs=[SMEM, SMEM, VMEM] + [VMEM] * len(parts),
        out_specs=VMEM,
        compiler_params=params(16),
        name=name,
    )(req, pos, stored, *parts)


def multiply(count, entry, left, right, acc):
    spare = acc.shape[0] - 1

    def group(g, carry):
        found = []
        for u in range(UNROLL):
            p = g * UNROLL + u
            i, j, o = entry(p)
            o = jnp.where(p < count, o, spare)
            found.append((o, jnp.dot(left[i], right[j], preferred_element_type=jnp.float32)))
        for o, term in found:
            acc[o] += term
        return carry

    lax.fori_loop(0, (count + UNROLL - 1) // UNROLL, group, 0)


def own_kernel(lay, prods, plan, counts, pos, stored_ref, *rest):
    parts = rest[: len(lay.stages)]
    acc, panel, sem = rest[len(lay.stages) :]
    copies = [pltpu.make_async_copy(stored_ref, panel.at[pl.ds(0, lay.stored)], sem.at[0])]
    for s, part in enumerate(parts):
        copies.append(
            pltpu.make_async_copy(part, panel.at[pl.ds(lay.stored + lay.start[s], lay.size(s))], sem.at[s + 1])
        )
    for copy in copies:
        copy.start()

    def zero(o, carry):
        acc[o] = jnp.zeros(acc.shape[1:], acc.dtype)
        return carry

    lax.fori_loop(0, acc.shape[0], zero, 0)
    for copy in copies:
        copy.wait()

    def where(which):
        lower = which >= lay.stored
        return jnp.where(lower, lay.stored + pos[jnp.where(lower, which - lay.stored, 0)], which)

    def entry(p):
        return where(plan[p]), where(plan[prods + p]), plan[2 * prods + p]

    multiply(counts[0], entry, panel, panel, acc)


def own_section(lay, plan_flat, counts, pos, stored, parts):
    block = stored.shape[-1]
    prods = plan_flat.shape[0] // 3
    return pl.pallas_call(
        functools.partial(own_kernel, lay, prods),
        out_shape=jax.ShapeDtypeStruct((OUTSLOTS + 1, block, block), jnp.float32),
        in_specs=[SMEM, SMEM, SMEM, VMEM] + [VMEM] * len(parts),
        out_specs=VMEM,
        scratch_shapes=[
            pltpu.VMEM((lay.stored + lay.total, block, block), stored.dtype),
            pltpu.SemaphoreType.DMA((len(parts) + 1,)),
        ],
        compiler_params=params(20),
        name="own_section",
    )(plan_flat, counts, pos, stored, *parts)


def next_kernel(lay, late, prods, plan, counts, slots_l, slots_r, pos, pos_r, acc, left_ref, self_ref, right_ref, *rest):
    parts = rest[: len(late)]
    out, left, right, sem = rest[len(late) :]
    copies = [
        pltpu.make_async_copy(left_ref, left.at[pl.ds(0, USED)], sem.at[0]),
        pltpu.make_async_copy(self_ref, left.at[pl.ds(USED, self_ref.shape[0])], sem.at[1]),
        pltpu.make_async_copy(right_ref, right.at[pl.ds(0, USED)], sem.at[2]),
    ]
    late_from = lay.start[late[0]] if late else lay.total
    for n, (s, part) in enumerate(zip(late, parts)):
        at = USED + lay.start[s] - late_from
        copies.append(pltpu.make_async_copy(part, right.at[pl.ds(at, lay.size(s))], sem.at[3 + n]))
    for copy in copies:
        copy.start()
    for copy in copies:
        copy.wait()
    self_from = lay.start[-2]

    def where(which, slot, table, first):
        lower = which >= lay.stored
        q = table[jnp.where(lower, which - lay.stored, 0)]
        return jnp.where(lower & (q >= first), USED + q - first, slot)

    def entry(p):
        i = where(plan[p], slots_l[p], pos, self_from)
        j = where(plan[prods + p], slots_r[p], pos_r, late_from)
        return i, j, plan[2 * prods + p]

    multiply(counts[1], entry, left, right, acc)

    def finish(o, carry):
        out[o] = acc[o].astype(out.dtype)
        return carry

    lax.fori_loop(0, OUTSLOTS, finish, 0)


def next_section(lay, late, plan_flat, counts, slots_l, slots_r, pos, pos_r, acc, left, self_part, right, parts):
    block = left.shape[-1]
    prods = plan_flat.shape[0] // 3
    late_size = sum(lay.size(s) for s in late)
    return pl.pallas_call(
        functools.partial(next_kernel, lay, late, prods),
        out_shape=jax.ShapeDtypeStruct((OUTSLOTS, block, block), left.dtype),
        in_specs=[SMEM] * 6 + [VMEM] * (4 + len(parts)),
        out_specs=VMEM,
        scratch_shapes=[
            pltpu.VMEM((USED + self_part.shape[0], block, block), left.dtype),
            pltpu.VMEM((USED + late_size, block, block), left.dtype),
            pltpu.SemaphoreType.DMA((3 + len(parts),)),
        ],
        compiler_params=params(20),
        name="next_section",
    )(plan_flat, counts, slots_l, slots_r, pos, pos_r, acc, left, self_part, right, *parts)


FLIGHT = 3
EARLY = 7


def body(upper_blocks, block_targets, product_plan, live_counts):
    stored = upper_blocks[0, 0]
    counts = live_counts[0, 0]
    plan = jnp.swapaxes(product_plan[0, 0], 1, 2)
    prods = plan.shape[2]
    plans = plan.reshape(2, 3 * prods)
    lay = Layout(stored.shape[0], lax.axis_size("col"))
    stages = range(len(lay.stages))
    early = list(stages)[:EARLY]
    late = list(stages)[EARLY:]
    col = lax.axis_index("col").astype(jnp.int32).reshape(1)

    first, pos, inv = first_stage(lay, block_targets[0, 0], col, stored)

    def exchange(s, send):
        parts = [
            moved(send[n * lay.cap : (n + 1) * lay.cap], "col", d) for n, d in enumerate(lay.stages[s])
        ]
        return parts[0] if len(parts) == 1 else jnp.concatenate(parts, axis=0)

    got = [exchange(0, first)]
    sends = [first, *rest_stages(lay, inv, stored)]
    reqs_l, reqs_r, slots_l, slots_r = wanted(2 * lay.stored, after(plans[1], got[0]), prods)
    asked_l = moved(reqs_l, "col", 1)
    asked_r = moved(reqs_r, "row", 1)
    pos_r = moved(pos, "row", -1)
    for s in stages[1:]:
        send = sends[s] if s < FLIGHT else after(sends[s], got[s - FLIGHT])
        got.append(exchange(s, send))
    right = moved(pick(lay, early, asked_r, pos, stored, [got[s] for s in early], "pick_right"), "row", -1)
    forwarded = [moved(got[s], "row", -1) for s in late]
    ready = list(stages)[:-1]
    left = moved(pick(lay, ready, asked_l, pos, stored, [got[s] for s in ready], "pick_left"), "col", -1)
    acc = own_section(lay, plans[0], counts, pos, stored, got)
    out = next_section(
        lay, late, plans[1], counts, slots_l, slots_r, pos, pos_r, acc, left, sends[-1], right, forwarded
    )
    return out[None, None]


def solution(mesh):
    placed = (
        P("row", "col", None, None, None),
        P("row", "col", None),
        P("row", "col", None, None, None),
        P("row", "col", None),
    )
    return jax.shard_map(
        body,
        mesh=mesh,
        in_specs=placed,
        out_specs=P("row", "col", None, None, None),
        check_vma=False,
    )
```

time: 271 us -> 94.3 us (0.35)
  the two profiles are of different devices: /device:TPU:31 before, /device:TPU:8 now
where the time goes in v1:
time: 94.3 us; the launch traced here: 93.3 us
  waiting for transfers between devices  47.8 us (51%)
  Pallas kernels  29.2 us (31%)
  starting transfers between devices  13.2 us (14%)
  local copies, waits for them, and re-layouts  2.86 us (3%)
    ppermute x12, waiting for transfers between devices, moved(): lax.ppermute(value, axis, [(s, (s + steps) % count) for s in range(count)])  47.8 us
    ppermute x12, starting transfers between devices, moved(): lax.ppermute(value, axis, [(s, (s + steps) % count) for s in range(count)])  13.2 us
    pallas_call x1, Pallas kernels, next_section(): pl.pallas_call(functools.partial(next_kernel, lay, late, prods), out_shap...  6.98 us
    pallas_call x1, Pallas kernels, wanted(): pl.pallas_call(functools.partial(wanted_kernel, prods), out_shape=(i32(US...  5.8 us
    pallas_call x1, Pallas kernels, rest_stages(): pl.pallas_call(functools.partial(rest_kernel, lay), out_shape=shapes, in_...  5.19 us
    pallas_call x2, Pallas kernels, pick(): pl.pallas_call(functools.partial(pick_kernel, lay, stages), out_shape=jax...  4.83 us
    pallas_call x1, Pallas kernels, own_section(): pl.pallas_call(functools.partial(own_kernel, lay, prods), out_shape=jax.S...  3.31 us
    pallas_call x1, Pallas kernels, first_stage(): pl.pallas_call(functools.partial(sort_kernel, lay), out_shape=(jax.ShapeD...  3.13 us
  transfers between devices with their start and end apart: 12, of which 6 were waited for; matrix products, arithmetic and copies ran while one was open for 1% of the time, Pallas kernels for 21%

profile of v1, /device:TPU:8, one launch (start us, length us, event | category | flops | bytes accessed | tf_op | source)
XLA Modules:
  0.0 93.3 jit_solution(9452483911610776190)
XLA Ops:
  0.0 1.6 %copy-done = bf16[1,1,63,128,128]{4,3,2,1,0:T(8,128)(2,1)S(1)} copy-done((bf16[1,1,63,128,128]{4,3,2,1,0:T(8,128)(2,1)S(1)}, bf16[1,1,63,128,128]{4,3,2,1,0:T(8,128)(2,1)}, u32[]{:S(2)}) %copy-start) | copy-done | bytes 2064408
  1.6 0.7 copy-done.4
  2.3 3.1 %sort_first.1 = (bf16[9,128,128]{2,1,0:T(8,128)(2,1)S(1)}, s32[63]{0:T(128)S(1)}, s32[63]{0:T(128)S(1)}) custom-call(s32[63]{0:T(128)S(1)} %bitcast.20, s32[1]{0:T(128)} %bitcast.4.col, bf16[63,128,128]{2,1,0:T(8,128)(2,1)S(1)} %bitcast.10), custom_call_target="tpu_custom_call" | custom-call | tf_op jit(solution)/shard_map/sort_first/pallas_call | solution.py:97
  5.4 0.1 collective-permute-start
  5.5 5.2 %flip_rest.1 = (bf16[9,128,128]{2,1,0:T(8,128)(2,1)S(1)}, bf16[9,128,128]{2,1,0:T(8,128)(2,1)S(1)}, bf16[9,128,128]{2,1,0:T(8,128)(2,1)S(1)}, bf16[9,128,128]{2,...) custom-call(s32[63]{0:T(128)S(1)} %get-tuple-element.28.inv, bf16[63,128,128]{2,1,0:T(8,128)(2,1)S(1)} %bitcast.11), custom_call_target="tpu_custom_call" | custom-call | tf_op jit(solution)/shard_map/flip_rest/pallas_call | solution.py:127
  10.7 3.5 %collective-permute-start.3 = (bf16[9,128,128]{2,1,0:T(8,128)(2,1)S(1)}, bf16[9,128,128]{2,1,0:T(8,128)(2,1)S(1)}, u32[]{:S(2)}, u32[]{:S(2)}) collective-permute-start(bf16[9,128,128]{2,1,0:T(8,128)(2,1)S(1)} %get-tuple-element.30), channel_id=1, source_target_pairs={{0,6},{1,7},{2,0},{3,1},{4,2},{5,3},{6,4},{7,5},{8,14},{9,15},{10,... | collective-permute-start | bytes 884744 | tf_op jit(solution)/shard_map/ppermute | solution.py:30
  14.1 0.0 collective-permute-start.2
  14.1 0.0 collective-permute-done.rest_0_
  14.1 6.3 %collective-permute-done.3.rest_2_ = bf16[9,128,128]{2,1,0:T(8,128)(2,1)S(1)} collective-permute-done((bf16[9,128,128]{2,1,0:T(8,128)(2,1)S(1)}, bf16[9,128,128]{2,1,0:T(8,128)(2,1)S(1)}, u32[]{:S(2)}, u32[]{:S(2)}) %collective-permute-start.3) | collective-permute-done | bytes 294944 | tf_op jit(solution)/shard_map/ppermute | solution.py:30
  20.5 4.4 %collective-permute-start.6 = (bf16[9,128,128]{2,1,0:T(8,128)(2,1)}, bf16[9,128,128]{2,1,0:T(8,128)(2,1)S(1)}, u32[]{:S(2)}, u32[]{:S(2)}) collective-permute-start(bf16[9,128,128]{2,1,0:T(8,128)(2,1)} %get-tuple-element.36), channel_id=1, source_target_pairs={{0,4},{1,5},{2,6},{3,7},{4,0},{5,1},{6,2},{7,3},{8,12},{9,13},{10,... | collective-permute-start | bytes 884744 | tf_op jit(solution)/shard_map/ppermute | solution.py:30
  24.9 4.0 %collective-permute-done.2.rest_1_ = bf16[9,128,128]{2,1,0:T(8,128)(2,1)S(1)} collective-permute-done((bf16[9,128,128]{2,1,0:T(8,128)(2,1)S(1)}, bf16[9,128,128]{2,1,0:T(8,128)(2,1)S(1)}, u32[]{:S(2)}, u32[]{:S(2)}) %collective-permute-start.2) | collective-permute-done | bytes 294944 | tf_op jit(solution)/shard_map/ppermute | solution.py:30
  28.9 0.6 collective-permute-start.5
  29.4 20.3 %collective-permute-done.4.rest_3_ = bf16[9,128,128]{2,1,0:T(8,128)(2,1)S(1)} collective-permute-done((bf16[9,128,128]{2,1,0:T(8,128)(2,1)S(1)}, bf16[9,128,128]{2,1,0:T(8,128)(2,1)S(1)}, u32[]{:S(2)}, u32[]{:S(2)}) %collective-permute-start.4) | collective-permute-done | bytes 294944 | tf_op jit(solution)/shard_map/ppermute | solution.py:30
  49.7 0.0 collective-permute-start.7
  49.7 0.6 slice_reduce_fusion
  50.3 5.8 %wanted.1 = (s32[24]{0:T(128)}, s32[24]{0:T(128)}, s32[128]{0:T(128)}, s32[128]{0:T(128)}) custom-call(s32[384]{0:T(512)} %bitcast.15), custom_call_target="tpu_custom_call" | custom-call | tf_op jit(solution)/shard_map/wanted/pallas_call | solution.py:166
  56.1 0.1 collective-permute-start.8
  56.1 1.5 %collective-permute-start.10 = (s32[24]{0:T(128)}, s32[24]{0:T(128)S(1)}, u32[]{:S(2)}, u32[]{:S(2)}) collective-permute-start(s32[24]{0:T(128)} %get-tuple-element.40), channel_id=1, source_target_pairs={{0,8},{8,16},{16,24},{24,0},{1,9},{9,17},{17,25},{25,1},{2,10},{10... | collective-permute-start | bytes 296 | tf_op jit(solution)/shard_map/ppermute | solution.py:30
  57.7 1.5 %collective-permute-done.8.req = s32[24]{0:T(128)S(1)} collective-permute-done((s32[24]{0:T(128)}, s32[24]{0:T(128)S(1)}, u32[]{:S(2)}, u32[]{:S(2)}) %collective-permute-start.8) | collective-permute-done | bytes 128 | tf_op jit(solution)/shard_map/ppermute | solution.py:30
  59.2 2.1 %collective-permute-done.5.rest_4_ = bf16[9,128,128]{2,1,0:T(8,128)(2,1)} collective-permute-done((bf16[9,128,128]{2,1,0:T(8,128)(2,1)}, bf16[9,128,128]{2,1,0:T(8,128)(2,1)}, u32[]{:S(2)}, u32[]{:S(2)}) %collective-permute-start.5) | collective-permute-done | bytes 294944 | tf_op jit(solution)/shard_map/ppermute | solution.py:30
  61.3 2.3 %pick_left.1 = bf16[24,128,128]{2,1,0:T(8,128)(2,1)S(1)} custom-call(s32[24]{0:T(128)S(1)} %collective-permute-done.8.req, s32[63]{0:T(128)S(1)} %get-tuple-element.27.pos, bf16[63,128,128]{2,1,0:T(8,128)(2,1)S(1)} %bitcast.12, bf16[9,128,128]{2,1,0:T(8,128)(2,1)S(1)} %collective-permute-done.rest_0_, ...), custom_call_target="tpu_custom_call" | custom-call | tf_op jit(solution)/shard_map/pick_left/pallas_call | solution.py:201
  63.5 0.0 copy-start.3
  63.6 0.1 collective-permute-start.9
  63.6 0.0 collective-permute-done.7.rest_6_
  63.6 2.5 %pick_right.1 = bf16[24,128,128]{2,1,0:T(8,128)(2,1)S(1)} custom-call(s32[24]{0:T(128)S(1)} %collective-permute-done.10.req, s32[63]{0:T(128)S(1)} %get-tuple-element.27.pos, bf16[63,128,128]{2,1,0:T(8,128)(2,1)S(1)} %bitcast.13, bf16[9,128,128]{2,1,0:T(8,128)(2,1)S(1)} %collective-permute-done.rest_0_, ...), custom_call_target="tpu_custom_call" | custom-call | tf_op jit(solution)/shard_map/pick_right/pallas_call | solution.py:201
  66.2 2.5 %collective-permute-start.11 = (bf16[24,128,128]{2,1,0:T(8,128)(2,1)S(1)}, bf16[24,128,128]{2,1,0:T(8,128)(2,1)S(1)}, u32[]{:S(2)}, u32[]{:S(2)}) collective-permute-start(bf16[24,128,128]{2,1,0:T(8,128)(2,1)S(1)} %pick_right.1), channel_id=1, source_target_pairs={{0,24},{8,0},{16,8},{24,16},{1,25},{9,1},{17,9},{25,17},{2,26},{10... | collective-permute-start | bytes 2359304 | tf_op jit(solution)/shard_map/ppermute | solution.py:30
  68.7 0.5 collective-permute-start.1
  69.2 3.3 %own_section.1.acc = f32[33,128,128]{2,1,0:T(8,128)S(1)} custom-call(s32[384]{0:T(512)S(1)} %bitcast.17, s32[2]{0:T(128)S(1)} %bitcast.18, s32[63]{0:T(128)S(1)} %get-tuple-element.27.pos, bf16[63,128,128]{2,1,0:T(8,128)(2,1)S(1)} %bitcast.14, bf16[9,128,128]{2,1,0:T(8,128)(2,1)S(1)} %collective-permute-done.rest_0_, ...), custom_call_target="tpu_custom_call" | custom-call | tf_op jit(solution)/shard_map/own_section/pallas_call | solution.py:260
  72.6 13.7 %collective-permute-done.1.pos_r = s32[63]{0:T(128)S(1)} collective-permute-done((s32[63]{0:T(128)S(1)}, s32[63]{0:T(128)S(1)}, u32[]{:S(2)}, u32[]{:S(2)}) %collective-permute-start.1) | collective-permute-done | bytes 284 | tf_op jit(solution)/shard_map/ppermute | solution.py:30
  86.2 0.0 collective-permute-done.9.left_ref
  86.2 0.0 collective-permute-done.11.right_ref
  86.3 7.0 %next_section.1 = bf16[32,128,128]{2,1,0:T(8,128)(2,1)} custom-call(s32[384]{0:T(512)S(1)} %bitcast.16, s32[2]{0:T(128)S(1)} %bitcast.19, s32[128]{0:T(128)S(1)} %copy-done.5, s32[128]{0:T(128)S(1)} %copy-done.6, s32[63]{0:T(128)S(1)} %get-tuple-element.27.pos, s32[63]{0:T(128)S(1)} %collective-permute-done.1.pos_r, f32[33,128,128]{2,1,0:T(8,128)S(1)} %own_section.1.acc, ...), custom_call_target="tpu_custom_call" | custom-call | tf_op jit(solution)/shard_map/next_section/pallas_call | solution.py:315
  (16 shorter events, 0.0 us)
Async XLA Ops:
  0.0 49.7 %copy-start.7 = (s32[1,1,2,128,3]{3,2,4,1,0:T(2,128)S(1)}, s32[1,1,2,128,3]{3,2,4,1,0:T(2,128)}, u32[]{:S(2)}) copy-start(s32[1,1,2,128,3]{3,2,4,1,0:T(2,128)} %param.6) | copy-start | bytes 9220
  0.0 1.6 %copy-start = (bf16[1,1,63,128,128]{4,3,2,1,0:T(8,128)(2,1)S(1)}, bf16[1,1,63,128,128]{4,3,2,1,0:T(8,128)(2,1)}, u32[]{:S(2)}) copy-start(bf16[1,1,63,128,128]{4,3,2,1,0:T(8,128)(2,1)} %param.4) | copy-start | bytes 6193156
  1.6 0.7 copy-start.4
  2.3 3.2 %copy-start.1 = (bf16[1,1,63,128,128]{4,3,2,1,0:T(8,128)(2,1)S(1)}, bf16[1,1,63,128,128]{4,3,2,1,0:T(8,128)(2,1)}, u32[]{:S(2)}) copy-start(bf16[1,1,63,128,128]{4,3,2,1,0:T(8,128)(2,1)} %param.4) | copy-start | bytes 6193156
  5.4 8.7 %collective-permute-start = (bf16[9,128,128]{2,1,0:T(8,128)(2,1)S(1)}, bf16[9,128,128]{2,1,0:T(8,128)(2,1)S(1)}, u32[]{:S(2)}, u32[]{:S(2)}) collective-permute-start(bf16[9,128,128]{2,1,0:T(8,128)(2,1)S(1)} %get-tuple-element.23), channel_id=1, source_target_pairs={{0,7},{1,0},{2,1},{3,2},{4,3},{5,4},{6,5},{7,6},{8,15},{9,8},{10,9... | collective-permute-start | bytes 884744 | tf_op jit(solution)/shard_map/ppermute | solution.py:30
  10.7 9.8 %collective-permute-start.3 = (bf16[9,128,128]{2,1,0:T(8,128)(2,1)S(1)}, bf16[9,128,128]{2,1,0:T(8,128)(2,1)S(1)}, u32[]{:S(2)}, u32[]{:S(2)}) collective-permute-start(bf16[9,128,128]{2,1,0:T(8,128)(2,1)S(1)} %get-tuple-element.30), channel_id=1, source_target_pairs={{0,6},{1,7},{2,0},{3,1},{4,2},{5,3},{6,4},{7,5},{8,14},{9,15},{10,... | collective-permute-start | bytes 884744 | tf_op jit(solution)/shard_map/ppermute | solution.py:30
  14.1 14.7 %collective-permute-start.2 = (bf16[9,128,128]{2,1,0:T(8,128)(2,1)S(1)}, bf16[9,128,128]{2,1,0:T(8,128)(2,1)S(1)}, u32[]{:S(2)}, u32[]{:S(2)}) collective-permute-start(bf16[9,128,128]{2,1,0:T(8,128)(2,1)S(1)} %get-tuple-element.29), channel_id=1, source_target_pairs={{0,2},{1,3},{2,4},{3,5},{4,6},{5,7},{6,0},{7,1},{8,10},{9,11},{10,... | collective-permute-start | bytes 884744 | tf_op jit(solution)/shard_map/ppermute | solution.py:30
  14.1 35.5 %collective-permute-start.4 = (bf16[9,128,128]{2,1,0:T(8,128)(2,1)S(1)}, bf16[9,128,128]{2,1,0:T(8,128)(2,1)S(1)}, u32[]{:S(2)}, u32[]{:S(2)}) collective-permute-start(bf16[9,128,128]{2,1,0:T(8,128)(2,1)S(1)} %get-tuple-element.32), channel_id=1, source_target_pairs={{0,3},{1,4},{2,5},{3,6},{4,7},{5,0},{6,1},{7,2},{8,11},{9,12},{10,... | collective-permute-start | bytes 884744 | tf_op jit(solution)/shard_map/ppermute | solution.py:30
  20.5 38.7 %collective-permute-start.6 = (bf16[9,128,128]{2,1,0:T(8,128)(2,1)}, bf16[9,128,128]{2,1,0:T(8,128)(2,1)S(1)}, u32[]{:S(2)}, u32[]{:S(2)}) collective-permute-start(bf16[9,128,128]{2,1,0:T(8,128)(2,1)} %get-tuple-element.36), channel_id=1, source_target_pairs={{0,4},{1,5},{2,6},{3,7},{4,0},{5,1},{6,2},{7,3},{8,12},{9,13},{10,... | collective-permute-start | bytes 884744 | tf_op jit(solution)/shard_map/ppermute | solution.py:30
  28.9 32.4 %collective-permute-start.5 = (bf16[9,128,128]{2,1,0:T(8,128)(2,1)}, bf16[9,128,128]{2,1,0:T(8,128)(2,1)}, u32[]{:S(2)}, u32[]{:S(2)}) collective-permute-start(bf16[9,128,128]{2,1,0:T(8,128)(2,1)} %get-tuple-element.34), channel_id=1, source_target_pairs={{0,5},{1,6},{2,7},{3,0},{4,1},{5,2},{6,3},{7,4},{8,13},{9,14},{10,... | collective-permute-start | bytes 884744 | tf_op jit(solution)/shard_map/ppermute | solution.py:30
  49.7 14.0 %collective-permute-start.7 = (bf16[9,128,128]{2,1,0:T(8,128)(2,1)}, bf16[9,128,128]{2,1,0:T(8,128)(2,1)}, u32[]{:S(2)}, u32[]{:S(2)}) collective-permute-start(bf16[9,128,128]{2,1,0:T(8,128)(2,1)} %get-tuple-element.38.self_ref), channel_id=1, source_target_pairs={{0,1},{1,2},{2,3},{3,4},{4,5},{5,6},{6,7},{7,0},{8,9},{9,10},{10,1... | collective-permute-start | bytes 884744 | tf_op jit(solution)/shard_map/ppermute | solution.py:30
  56.1 3.1 %collective-permute-start.8 = (s32[24]{0:T(128)}, s32[24]{0:T(128)S(1)}, u32[]{:S(2)}, u32[]{:S(2)}) collective-permute-start(s32[24]{0:T(128)} %get-tuple-element.39), channel_id=1, source_target_pairs={{0,1},{1,2},{2,3},{3,4},{4,5},{5,6},{6,7},{7,0},{8,9},{9,10},{10,1... | collective-permute-start | bytes 296 | tf_op jit(solution)/shard_map/ppermute | solution.py:30
  56.1 7.5 %collective-permute-start.10 = (s32[24]{0:T(128)}, s32[24]{0:T(128)S(1)}, u32[]{:S(2)}, u32[]{:S(2)}) collective-permute-start(s32[24]{0:T(128)} %get-tuple-element.40), channel_id=1, source_target_pairs={{0,8},{8,16},{16,24},{24,0},{1,9},{9,17},{17,25},{25,1},{2,10},{10... | collective-permute-start | bytes 296 | tf_op jit(solution)/shard_map/ppermute | solution.py:30
  63.5 5.7 %copy-start.3 = (s32[1,1,2]{2,1,0:T(1,128)S(1)}, s32[1,1,2]{2,1,0:T(1,128)}, u32[]{:S(2)}) copy-start(s32[1,1,2]{2,1,0:T(1,128)} %param.7) | copy-start | bytes 28
  63.6 22.7 %collective-permute-start.9 = (bf16[24,128,128]{2,1,0:T(8,128)(2,1)S(1)}, bf16[24,128,128]{2,1,0:T(8,128)(2,1)S(1)}, u32[]{:S(2)}, u32[]{:S(2)}) collective-permute-start(bf16[24,128,128]{2,1,0:T(8,128)(2,1)S(1)} %pick_left.1), channel_id=1, source_target_pairs={{0,7},{1,0},{2,1},{3,2},{4,3},{5,4},{6,5},{7,6},{8,15},{9,8},{10,9... | collective-permute-start | bytes 2359304 | tf_op jit(solution)/shard_map/ppermute | solution.py:30
  66.2 20.1 %collective-permute-start.11 = (bf16[24,128,128]{2,1,0:T(8,128)(2,1)S(1)}, bf16[24,128,128]{2,1,0:T(8,128)(2,1)S(1)}, u32[]{:S(2)}, u32[]{:S(2)}) collective-permute-start(bf16[24,128,128]{2,1,0:T(8,128)(2,1)S(1)} %pick_right.1), channel_id=1, source_target_pairs={{0,24},{8,0},{16,8},{24,16},{1,25},{9,1},{17,9},{25,17},{2,26},{10... | collective-permute-start | bytes 2359304 | tf_op jit(solution)/shard_map/ppermute | solution.py:30
  68.7 17.5 %collective-permute-start.1 = (s32[63]{0:T(128)S(1)}, s32[63]{0:T(128)S(1)}, u32[]{:S(2)}, u32[]{:S(2)}) collective-permute-start(s32[63]{0:T(128)S(1)} %get-tuple-element.27.pos), channel_id=1, source_target_pairs={{0,24},{8,0},{16,8},{24,16},{1,25},{9,1},{17,9},{25,17},{2,26},{10... | collective-permute-start | bytes 764 | tf_op jit(solution)/shard_map/ppermute | solution.py:30
  69.2 17.0 %copy-start.2 = (s32[3,128]{1,0:T(4,128)S(1)}, s32[3,128]{1,0:T(4,128)}, u32[]{:S(2)}) copy-start(s32[3,128]{1,0:T(4,128)} %get-tuple-element.42) | copy-start | bytes 4612
  69.2 17.0 %copy-start.5 = (s32[128]{0:T(128)S(1)}, s32[128]{0:T(128)}, u32[]{:S(2)}) copy-start(s32[128]{0:T(128)} %get-tuple-element.25.slots_l) | copy-start | bytes 1540
  69.2 17.0 %copy-start.6 = (s32[128]{0:T(128)S(1)}, s32[128]{0:T(128)}, u32[]{:S(2)}) copy-start(s32[128]{0:T(128)} %get-tuple-element.26.slots_r) | copy-start | bytes 1540

commit v2 on v1

v2 whole, which is shorter than its diff:
```python
import functools

import jax
import jax.numpy as jnp
from jax import lax
from jax.experimental import pallas as pl
from jax.experimental.pallas import tpu as pltpu
from jax.sharding import PartitionSpec as P

OUTSLOTS = 32
USED = 24
UNROLL = 8
FIRST = 2
LEFT_PIECES = 1
RIGHT_PIECES = 1
FIRST_MIB = 62
MIB = 1 << 20

SMEM = pl.BlockSpec(memory_space=pltpu.SMEM)
VMEM = pl.BlockSpec(memory_space=pltpu.VMEM)
HBM = pl.BlockSpec(memory_space=pltpu.HBM)


def cost(us):
    return pl.CostEstimate(flops=0, bytes_accessed=int(us * 3.5e6), transcendentals=0)


def i32(*shape):
    return jax.ShapeDtypeStruct(shape, jnp.int32)


def params(mib):
    return pltpu.CompilerParams(vmem_limit_bytes=mib * MIB)


def moved(value, axis, steps):
    count = lax.axis_size(axis)
    return lax.ppermute(value, axis, [(s, (s + steps) % count) for s in range(count)])


def after(value, *needed):
    return lax.optimization_barrier((value, *needed))[0]


class Order:
    def __init__(self, token):
        self.token = token

    def gate(self, value):
        value, self.token = lax.optimization_barrier((value, self.token))
        return value


class Layout:
    def __init__(self, stored, cols):
        self.stored = stored
        self.cols = cols
        self.cap = (stored + cols - 2) // (cols - 1)
        half = cols // 2
        others = [d for d in range(2, cols) if d != half]
        others.sort(key=lambda d: (half - abs(d - half), d))
        others = others[1:3] + others[:1] + others[3:]
        pieces = min(5, len(others))
        cuts = [len(others) * i // pieces for i in range(pieces + 1)]
        self.stages = [others[a:b] for a, b in zip(cuts, cuts[1:])] + [[1], [half]]
        self.base = [0] * cols
        self.start = []
        at = 0
        for stage in self.stages:
            self.start.append(at)
            for d in stage:
                self.base[d] = at
                at += self.cap
        self.total = at
        self.start.append(at)
        self.self_stage = self.stages.index([1])

    def size(self, s):
        return self.start[s + 1] - self.start[s]


def offset_of(lay, tgt, k, me):
    d = tgt[k] - me
    return jnp.where(d < 0, d + lay.cols, d)


def first_kernel(lay, tgt, col, stored_ref, *rest):
    outs, (buf, found, sem) = rest[:FIRST], rest[FIRST:]
    goals = []
    for n, offset in enumerate(d for stage in lay.stages[:FIRST] for d in stage):
        goal = col[0] + offset
        goals.append(jnp.where(goal >= lay.cols, goal - lay.cols, goal))
    at = [jnp.int32(n * lay.cap) for n in range(len(goals))]
    for k in range(lay.stored):
        target = tgt[k]
        for n, goal in enumerate(goals):
            hit = target == goal
            found[jnp.where(hit, at[n], lay.total)] = k
            at[n] = at[n] + hit.astype(jnp.int32)
    total = lay.start[FIRST]
    for j in range(total):
        pltpu.make_async_copy(stored_ref.at[found[j]], buf.at[j], sem).start()
    pltpu.make_async_copy(buf, buf, sem).wait()
    for s, out in enumerate(outs):
        for j in range(lay.size(s)):
            out[j] = buf[lay.start[s] + j].T


def first_stage(lay, targets, col, stored):
    block = stored.shape[-1]
    return pl.pallas_call(
        functools.partial(first_kernel, lay),
        out_shape=tuple(jax.ShapeDtypeStruct((lay.size(s), block, block), stored.dtype) for s in range(FIRST)),
        in_specs=[SMEM, SMEM, HBM],
        out_specs=(VMEM,) * FIRST,
        scratch_shapes=[
            pltpu.VMEM((lay.start[FIRST], block, block), stored.dtype),
            pltpu.SMEM((lay.total + 1,), jnp.int32),
            pltpu.SemaphoreType.DMA,
        ],
        compiler_params=params(FIRST_MIB),
        name="first_stage",
    )(targets, col, stored)


def rest_kernel(lay, tgt, col, ids, stored_ref, *rest):
    outs, pos, inv, cnt = rest[:-3], rest[-3], rest[-2], rest[-1]
    for d in range(lay.cols):
        cnt[d] = lay.base[d]

    def place(k, carry):
        d = offset_of(lay, tgt, k, col[0])
        q = cnt[d]
        cnt[d] = q + 1
        pos[k] = q
        inv[q] = k
        return carry

    lax.fori_loop(0, lay.stored, place, 0)
    for s in range(FIRST, len(lay.stages)):

        def flip(j, carry, s=s):
            outs[s - FIRST][j] = stored_ref[inv[lay.start[s] + j]].T
            return carry

        lax.fori_loop(0, lay.size(s), flip, 0, unroll=lay.size(s) % 3 == 0 and 3 or 1)
    note = outs[lay.self_stage - FIRST]
    rows, block = ids.shape
    for row in range(rows):
        line = ids[row : row + 1, :].astype(jnp.float32)
        note[lay.size(lay.self_stage), row * 16 : row * 16 + 16, :] = jnp.broadcast_to(line, (16, block)).astype(note.dtype)


def rest_stages(lay, targets, col, ids, stored):
    block = stored.shape[-1]
    shapes = tuple(
        jax.ShapeDtypeStruct((lay.size(s) + (s == lay.self_stage), block, block), stored.dtype)
        for s in range(FIRST, len(lay.stages))
    )
    return pl.pallas_call(
        functools.partial(rest_kernel, lay),
        out_shape=shapes + (i32(lay.stored),),
        in_specs=[SMEM, SMEM, VMEM, VMEM],
        out_specs=(VMEM,) * len(shapes) + (SMEM,),
        scratch_shapes=[pltpu.SMEM((lay.total,), jnp.int32), pltpu.SMEM((lay.cols,), jnp.int32)],
        compiler_params=params(12),
        cost_estimate=cost(0.01),
        name="rest_stages",
    )(targets, col, ids, stored)


def wanted_kernel(prods, plan, reqs_r, slots_l, slots_r, seen_l, seen_r):
    def clear(i, carry):
        seen_l[i] = -1
        seen_r[i] = -1
        return carry

    lax.fori_loop(0, seen_l.shape[0], clear, 0, unroll=6 if seen_l.shape[0] % 6 == 0 else 1)
    for i in range(USED):
        reqs_r[i] = 0

    def step(p, counts):
        sides = ((slots_l, seen_l), (slots_r, seen_r))
        found = [plan[side * prods + p] for side in range(2)]
        known = [seen[which] for (_, seen), which in zip(sides, found)]
        slot = [jnp.where(k < 0, n, k) for k, n in zip(known, counts)]
        for (slots, seen), which, at in zip(sides, found, slot):
            seen[which] = at
            slots[p] = at
        reqs_r[slot[1]] = found[1]
        return tuple(n + (k < 0).astype(jnp.int32) for k, n in zip(known, counts))

    lax.fori_loop(0, prods, step, (jnp.int32(0), jnp.int32(0)), unroll=4)


def wanted(panel_size, plan_flat, prods):
    return pl.pallas_call(
        functools.partial(wanted_kernel, prods),
        out_shape=(i32(USED), i32(prods), i32(prods)),
        in_specs=[SMEM],
        out_specs=(SMEM,) * 3,
        scratch_shapes=[pltpu.SMEM((panel_size,), jnp.int32)] * 2,
        cost_estimate=cost(0.01),
        name="wanted",
    )(plan_flat)


def asked_kernel(ids, reqs, seen):
    def clear(i, carry):
        seen[i] = 0
        return carry

    lax.fori_loop(0, seen.shape[0], clear, 0, unroll=6 if seen.shape[0] % 6 == 0 else 1)

    def step(p, n):
        which = ids[p]
        known = seen[which]
        reqs[n] = which
        seen[which] = 1
        return n + 1 - known

    lax.fori_loop(0, ids.shape[0], step, jnp.int32(0), unroll=4)


def asked(panel_size, ids):
    return pl.pallas_call(
        asked_kernel,
        out_shape=i32(USED + 1),
        in_specs=[SMEM],
        out_specs=SMEM,
        scratch_shapes=[pltpu.SMEM((panel_size,), jnp.int32)],
        name="asked",
    )(ids)


def pick_kernel(lay, stages, pieces, req, pos, stored_ref, *rest):
    parts, outs = rest[: len(stages)], rest[len(stages) :]
    size = USED // pieces
    for piece, out in enumerate(outs):

        def step(n, carry, piece=piece, out=out):
            which = req[piece * size + n]
            lower = which >= lay.stored
            q = pos[jnp.where(lower, which - lay.stored, 0)]

            @pl.when(jnp.logical_not(lower))
            def _():
                out[n] = stored_ref[which]

            for s, part in zip(stages, parts):

                @pl.when(lower & (q >= lay.start[s]) & (q < lay.start[s + 1]))
                def _(s=s, part=part):
                    out[n] = part[q - lay.start[s]]

            return carry

        lax.fori_loop(0, size, step, 0)


def pick(lay, stages, pieces, req, pos, stored, parts, name):
    block = stored.shape[-1]
    return pl.pallas_call(
        functools.partial(pick_kernel, lay, stages, pieces),
        out_shape=(jax.ShapeDtypeStruct((USED // pieces, block, block), stored.dtype),) * pieces,
        in_specs=[SMEM, SMEM, VMEM] + [VMEM] * len(parts),
        out_specs=(VMEM,) * pieces,
        compiler_params=params(16),
        name=name,
    )(req, pos, stored, *parts)


def multiply(count, entry, left, right, acc):
    spare = acc.shape[0] - 1

    def group(g, carry):
        found = []
        for u in range(UNROLL):
            p = g * UNROLL + u
            i, j, o = entry(p)
            o = jnp.where(p < count, o, spare)
            found.append((o, jnp.dot(left[i], right[j], preferred_element_type=jnp.float32)))
        for o, term in found:
            acc[o] += term
        return carry

    lax.fori_loop(0, (count + UNROLL - 1) // UNROLL, group, 0)


def own_kernel(lay, prods, plan, counts, pos, stored_ref, *rest):
    parts = rest[: len(lay.stages)]
    acc, panel, sem = rest[len(lay.stages) :]
    copies = [pltpu.make_async_copy(stored_ref, panel.at[pl.ds(0, lay.stored)], sem.at[0])]
    for s, part in enumerate(parts):
        copies.append(
            pltpu.make_async_copy(
                part.at[pl.ds(0, lay.size(s))], panel.at[pl.ds(lay.stored + lay.start[s], lay.size(s))], sem.at[s + 1]
            )
        )
    for copy in copies:
        copy.start()

    def zero(o, carry):
        acc[o] = jnp.zeros(acc.shape[1:], acc.dtype)
        return carry

    lax.fori_loop(0, acc.shape[0], zero, 0)
    for copy in copies:
        copy.wait()

    def where(which):
        lower = which >= lay.stored
        return jnp.where(lower, lay.stored + pos[jnp.where(lower, which - lay.stored, 0)], which)

    def entry(p):
        return where(plan[p]), where(plan[prods + p]), plan[2 * prods + p]

    multiply(counts[0], entry, panel, panel, acc)


def own_section(lay, plan_flat, counts, pos, stored, parts):
    block = stored.shape[-1]
    prods = plan_flat.shape[0] // 3
    return pl.pallas_call(
        functools.partial(own_kernel, lay, prods),
        out_shape=jax.ShapeDtypeStruct((OUTSLOTS + 1, block, block), jnp.float32),
        in_specs=[SMEM, SMEM, SMEM, VMEM] + [VMEM] * len(parts),
        out_specs=VMEM,
        scratch_shapes=[
            pltpu.VMEM((lay.stored + lay.total, block, block), stored.dtype),
            pltpu.SemaphoreType.DMA((len(parts) + 1,)),
        ],
        compiler_params=params(20),
        cost_estimate=cost(0.01),
        name="own_section",
    )(plan_flat, counts, pos, stored, *parts)


def next_kernel(lay, late, prods, token, plan, counts, slots_l, slots_r, pos, pos_r, acc, self_ref, *rest):
    lefts, rights, parts = rest[:LEFT_PIECES], rest[LEFT_PIECES : LEFT_PIECES + RIGHT_PIECES], rest[LEFT_PIECES + RIGHT_PIECES : -4]
    out, left, right, sem = rest[-4:]
    late_from = lay.start[late[0]] if late else lay.total
    moves = [(self_ref, left, USED, lay.size(lay.self_stage))]
    moves += [(part, left, n * part.shape[0], part.shape[0]) for n, part in enumerate(lefts)]
    moves += [(part, right, n * part.shape[0], part.shape[0]) for n, part in enumerate(rights)]
    moves += [(part, right, USED + lay.start[s] - late_from, lay.size(s)) for s, part in zip(late, parts)]
    copies = [
        pltpu.make_async_copy(part.at[pl.ds(0, size)], whole.at[pl.ds(at, size)], sem.at[n])
        for n, (part, whole, at, size) in enumerate(moves)
    ]
    for copy in copies:
        copy.start()
    for copy in copies:
        copy.wait()

    def where(which, slot, table, first, last):
        lower = which >= lay.stored
        q = table[jnp.where(lower, which - lay.stored, 0)]
        return jnp.where(lower & (q >= first) & (q < last), USED + q - first, slot)

    def entry(p):
        own = lay.self_stage
        i = where(plan[p], slots_l[p], pos, lay.start[own], lay.start[own + 1])
        j = where(plan[prods + p], slots_r[p], pos_r, late_from, lay.total)
        return i, j, plan[2 * prods + p]

    multiply(counts[1], entry, left, right, acc)

    def finish(o, carry):
        out[o] = acc[o].astype(out.dtype)
        return carry

    lax.fori_loop(0, OUTSLOTS, finish, 0)


def next_section(lay, late, token, plan_flat, counts, slots_l, slots_r, pos, pos_r, acc, left, self_part, right, parts):
    block = self_part.shape[-1]
    prods = plan_flat.shape[0] // 3
    late_size = sum(lay.size(s) for s in late)
    return pl.pallas_call(
        functools.partial(next_kernel, lay, late, prods),
        out_shape=jax.ShapeDtypeStruct((OUTSLOTS, block, block), self_part.dtype),
        in_specs=[SMEM] * 7 + [VMEM] * (2 + len(left) + len(right) + len(parts)),
        out_specs=VMEM,
        scratch_shapes=[
            pltpu.VMEM((USED + lay.size(lay.self_stage), block, block), self_part.dtype),
            pltpu.VMEM((USED + late_size, block, block), self_part.dtype),
            pltpu.SemaphoreType.DMA((1 + len(left) + len(right) + len(parts),)),
        ],
        compiler_params=params(20),
        cost_estimate=cost(0.01),
        name="next_section",
    )(token, plan_flat, counts, slots_l, slots_r, pos, pos_r, acc, self_part, *left, *right, *parts)


FLIGHT = 2
EARLY = 6


def body(upper_blocks, block_targets, product_plan, live_counts):
    stored = upper_blocks[0, 0]
    targets = block_targets[0, 0]
    counts = live_counts[0, 0]
    plan = jnp.swapaxes(product_plan[0, 0], 1, 2)
    prods = plan.shape[2]
    plans = plan.reshape(2, 3 * prods)
    lay = Layout(stored.shape[0], lax.axis_size("col"))
    stages = list(range(len(lay.stages)))
    early, late = stages[:EARLY], stages[EARLY:]
    col = lax.axis_index("col").astype(jnp.int32).reshape(1)

    def exchange(s, send):
        if len(lay.stages[s]) == 1:
            return moved(send, "col", lay.stages[s][0])
        parts = [
            moved(send[n * lay.cap : (n + 1) * lay.cap], "col", d) for n, d in enumerate(lay.stages[s])
        ]
        return jnp.concatenate(parts, axis=0)

    order = Order(col)
    sends = list(first_stage(lay, targets, col, stored))
    got = [exchange(s, sends[s]) for s in range(FIRST)]
    *rest, pos = rest_stages(lay, targets, col, plans[1, :prods].reshape(-1, stored.shape[-1]), order.gate(stored))
    sends += rest
    got += [exchange(s, sends[s]) for s in stages[FIRST:4]]
    reqs_r, slots_l, slots_r = order.gate(wanted(2 * lay.stored, order.gate(plans[1]), prods))
    asked_r = moved(reqs_r, "row", 1)
    pos_r = moved(pos, "row", -1)
    got += [exchange(s, sends[s]) for s in stages[4:-1]]
    for s in stages[:3]:
        got[s] = order.gate(got[s])
    asked_r = order.gate(asked_r)
    for s in stages[3:-2]:
        got[s] = order.gate(got[s])
    got.append(exchange(stages[-1], order.gate(sends[-1])))
    got[-2] = order.gate(got[-2])
    rows = prods // stored.shape[-1]
    ids = got[lay.self_stage][-1, : 16 * rows : 16].reshape(-1).astype(jnp.int32)
    asked_l = order.gate(asked(2 * lay.stored, order.gate(ids)))
    picked = order.gate(pick(lay, early, RIGHT_PIECES, asked_r, pos, stored, [got[s] for s in early], "pick_right"))
    right = [moved(piece, "row", -1) for piece in picked]
    got[-1] = order.gate(got[-1])
    forwarded = [moved(got[s], "row", -1) for s in late]
    ready = [s for s in stages if s != lay.self_stage]
    picked = pick(lay, ready, LEFT_PIECES, order.gate(asked_l), pos, stored, [got[s] for s in ready], "pick_left")
    left = [moved(piece, "col", -1) for piece in order.gate(picked)]
    right = order.gate(right)
    acc = own_section(lay, order.gate(plans[0]), counts, pos, stored, got)
    out = next_section(
        lay, late, order.token, plans[1], counts, slots_l, slots_r, pos, pos_r, acc, left, sends[lay.self_stage], right, forwarded
    )
    return out[None, None]


def solution(mesh):
    placed = (
        P("row", "col", None, None, None),
        P("row", "col", None),
        P("row", "col", None, None, None),
        P("row", "col", None),
    )
    return jax.shard_map(
        body,
        mesh=mesh,
        in_specs=placed,
        out_specs=P("row", "col", None, None, None),
        check_vma=False,
    )
```

time: 94.3 us -> 82.9 us (0.88)
  the two profiles are of different devices: /device:TPU:8 before, /device:TPU:0 now
where the time goes in v2:
time: 82.9 us; the launch traced here: 82.7 us
  starting transfers between devices  28.6 us (34%)
  waiting for transfers between devices  25.4 us (31%)
  Pallas kernels  23 us (28%)
  local copies, waits for them, and re-layouts  4.26 us (5%)
  other arithmetic  1.17 us (1%)
    ppermute x12, starting transfers between devices, moved(): lax.ppermute(value, axis, [(s, (s + steps) % count) for s in range(count)])  28.6 us
    ppermute x12, waiting for transfers between devices, moved(): lax.ppermute(value, axis, [(s, (s + steps) % count) for s in range(count)])  25.4 us
    pallas_call x2, Pallas kernels, pick(): pl.pallas_call(functools.partial(pick_kernel, lay, stages, pieces), out_s...  4.59 us
    pallas_call x1, Pallas kernels, next_section(): pl.pallas_call(functools.partial(next_kernel, lay, late, prods), out_shap...  4.2 us
    pallas_call x1, Pallas kernels, rest_stages(): pl.pallas_call(functools.partial(rest_kernel, lay), out_shape=shapes + (i...  3.8 us
    pallas_call x1, Pallas kernels, first_stage(): pl.pallas_call(functools.partial(first_kernel, lay), out_shape=tuple((jax...  3.08 us
    unnamed x20, local copies, waits for them, and re-layouts  2.99 us
    pallas_call x1, Pallas kernels, own_section(): pl.pallas_call(functools.partial(own_kernel, lay, prods), out_shape=jax.S...  2.89 us
  transfers between devices with their start and end apart: 12, of which 7 were waited for; matrix products, arithmetic and copies ran while one was open for 3% of the time, Pallas kernels for 19%

profile of v2, /device:TPU:0, one launch (start us, length us, event | category | flops | bytes accessed | tf_op | source)
XLA Modules:
  0.0 82.7 jit_solution(16053673317028207336)
XLA Ops:
  0.0 3.1 %first_stage.1 = (bf16[9,128,128]{2,1,0:T(8,128)(2,1)}, bf16[9,128,128]{2,1,0:T(8,128)(2,1)}) custom-call(s32[63]{0:T(128)} %bitcast.25, s32[1]{0:T(128)} %bitcast.4.col.token, bf16[63,128,128]{2,1,0:T(8,128)(2,1)} %bitcast.15), custom_call_target="tpu_custom_call" | custom-call | tf_op jit(solution)/shard_map/first_stage/pallas_call | solution.py:111
  3.1 3.1 %collective-permute-start.3 = (bf16[9,128,128]{2,1,0:T(8,128)(2,1)}, bf16[9,128,128]{2,1,0:T(8,128)(2,1)S(1)}, u32[]{:S(2)}, u32[]{:S(2)}) collective-permute-start(bf16[9,128,128]{2,1,0:T(8,128)(2,1)} %get-tuple-element.66), channel_id=1, source_target_pairs={{0,2},{1,3},{2,4},{3,5},{4,6},{5,7},{6,0},{7,1},{8,10},{9,11},{10,... | collective-permute-start | bytes 884744 | tf_op jit(solution)/shard_map/ppermute | solution.py:38
  6.2 2.1 %collective-permute-start.2 = (bf16[9,128,128]{2,1,0:T(8,128)(2,1)}, bf16[9,128,128]{2,1,0:T(8,128)(2,1)S(1)}, u32[]{:S(2)}, u32[]{:S(2)}) collective-permute-start(bf16[9,128,128]{2,1,0:T(8,128)(2,1)} %get-tuple-element.65), channel_id=1, source_target_pairs={{0,6},{1,7},{2,0},{3,1},{4,2},{5,3},{6,4},{7,5},{8,14},{9,15},{10,... | collective-permute-start | bytes 884744 | tf_op jit(solution)/shard_map/ppermute | solution.py:38
  8.3 0.7 slice.22.ids
  8.9 1.6 %copy-done = bf16[1,1,63,128,128]{4,3,2,1,0:T(8,128)(2,1)S(1)} copy-done((bf16[1,1,63,128,128]{4,3,2,1,0:T(8,128)(2,1)S(1)}, bf16[1,1,63,128,128]{4,3,2,1,0:T(8,128)(2,1)}, u32[]{:S(2)}) %copy-start) | copy-done | bytes 2064408
  10.5 0.7 copy-done.4
  11.2 3.8 %rest_stages.1 = (bf16[9,128,128]{2,1,0:T(8,128)(2,1)}, bf16[9,128,128]{2,1,0:T(8,128)(2,1)}, bf16[9,128,128]{2,1,0:T(8,128)(2,1)}, bf16[10,128,128]{2,1,0:T(8,1...) custom-call(s32[63]{0:T(128)S(1)} %bitcast.26, s32[1]{0:T(128)} %bitcast.4.col.token, s32[1,128]{1,0:T(1,128)S(1)} %slice.22.ids, ...), custom_call_target="tpu_custom_call" | custom-call | bytes 35000 | tf_op jit(solution)/shard_map/rest_stages/pallas_call | solution.py:160
  15.0 0.7 copy-done.8
  15.7 0.8 %collective-permute-start.1 = (bf16[9,128,128]{2,1,0:T(8,128)(2,1)}, bf16[9,128,128]{2,1,0:T(8,128)(2,1)S(1)}, u32[]{:S(2)}, u32[]{:S(2)}) collective-permute-start(bf16[9,128,128]{2,1,0:T(8,128)(2,1)} %get-tuple-element.64), channel_id=1, source_target_pairs={{0,7},{1,0},{2,1},{3,2},{4,3},{5,4},{6,5},{7,6},{8,15},{9,8},{10,9... | collective-permute-start | bytes 884744 | tf_op jit(solution)/shard_map/ppermute | solution.py:38
  16.6 2.6 %collective-permute-start.5 = (bf16[9,128,128]{2,1,0:T(8,128)(2,1)}, bf16[9,128,128]{2,1,0:T(8,128)(2,1)S(1)}, u32[]{:S(2)}, u32[]{:S(2)}) collective-permute-start(bf16[9,128,128]{2,1,0:T(8,128)(2,1)} %get-tuple-element.79), channel_id=1, source_target_pairs={{0,5},{1,6},{2,7},{3,0},{4,1},{5,2},{6,3},{7,4},{8,13},{9,14},{10,... | collective-permute-start | bytes 884744 | tf_op jit(solution)/shard_map/ppermute | solution.py:38
  19.2 0.6 collective-permute-start.6
  19.8 0.6 slice_reduce_fusion
  20.4 2.6 %wanted.1 = (s32[24]{0:T(128)}, s32[128]{0:T(128)}, s32[128]{0:T(128)}) custom-call(s32[384]{0:T(512)} %bitcast.20), custom_call_target="tpu_custom_call" | custom-call | bytes 35000 | tf_op jit(solution)/shard_map/wanted/pallas_call | solution.py:197
  23.0 1.7 %collective-permute-start = (s32[24]{0:T(128)}, s32[24]{0:T(128)S(1)}, u32[]{:S(2)}, u32[]{:S(2)}) collective-permute-start(s32[24]{0:T(128)} %get-tuple-element.62), channel_id=1, source_target_pairs={{0,8},{8,16},{16,24},{24,0},{1,9},{9,17},{17,25},{25,1},{2,10},{10... | collective-permute-start | bytes 296 | tf_op jit(solution)/shard_map/ppermute | solution.py:38
  24.7 1.9 %collective-permute-done.1.rest_2_ = bf16[9,128,128]{2,1,0:T(8,128)(2,1)S(1)} collective-permute-done((bf16[9,128,128]{2,1,0:T(8,128)(2,1)}, bf16[9,128,128]{2,1,0:T(8,128)(2,1)S(1)}, u32[]{:S(2)}, u32[]{:S(2)}) %collective-permute-start.1) | collective-permute-done | bytes 294944 | tf_op jit(solution)/shard_map/ppermute | solution.py:38
  26.6 1.0 %collective-permute-done.req = s32[24]{0:T(128)S(1)} collective-permute-done((s32[24]{0:T(128)}, s32[24]{0:T(128)S(1)}, u32[]{:S(2)}, u32[]{:S(2)}) %collective-permute-start) | collective-permute-done | bytes 128 | tf_op jit(solution)/shard_map/ppermute | solution.py:38
  27.6 5.7 %collective-permute-done.4.rest_3_ = bf16[9,128,128]{2,1,0:T(8,128)(2,1)S(1)} collective-permute-done((bf16[9,128,128]{2,1,0:T(8,128)(2,1)}, bf16[9,128,128]{2,1,0:T(8,128)(2,1)S(1)}, u32[]{:S(2)}, u32[]{:S(2)}) %collective-permute-start.4) | collective-permute-done | bytes 294944 | tf_op jit(solution)/shard_map/ppermute | solution.py:38
  33.3 5.1 %collective-permute-done.5.rest_4_ = bf16[9,128,128]{2,1,0:T(8,128)(2,1)S(1)} collective-permute-done((bf16[9,128,128]{2,1,0:T(8,128)(2,1)}, bf16[9,128,128]{2,1,0:T(8,128)(2,1)S(1)}, u32[]{:S(2)}, u32[]{:S(2)}) %collective-permute-start.5) | collective-permute-done | bytes 294944 | tf_op jit(solution)/shard_map/ppermute | solution.py:38
  38.4 8.6 %collective-permute-start.8 = (bf16[9,128,128]{2,1,0:T(8,128)(2,1)}, bf16[9,128,128]{2,1,0:T(8,128)(2,1)}, u32[]{:S(2)}, u32[]{:S(2)}) collective-permute-start(bf16[9,128,128]{2,1,0:T(8,128)(2,1)} %copy-done.8), channel_id=1, source_target_pairs={{0,4},{1,5},{2,6},{3,7},{4,0},{5,1},{6,2},{7,3},{8,12},{9,13},{10,... | collective-permute-start | bytes 884744 | tf_op jit(solution)/shard_map/ppermute | solution.py:38
  47.0 1.2 %bitcast_convert_fusion.ids = s32[128]{0:T(128)} fusion(bf16[10,128,128]{2,1,0:T(8,128)(2,1)} %collective-permute-done.6.rest_5_), kind=kLoop, calls=%fused_computation.2 | loop fusion | flops 128 | bytes 768 | tf_op jit(solution)/shard_map/convert_element_type | solution.py:438
  48.2 1.8 %asked.1.req = s32[25]{0:T(128)} custom-call(s32[128]{0:T(128)} %bitcast_convert_fusion.ids), custom_call_target="tpu_custom_call" | custom-call | tf_op jit(solution)/shard_map/asked/pallas_call | solution.py:226
  50.0 2.3 %pick_right.1 = bf16[24,128,128]{2,1,0:T(8,128)(2,1)S(1)} custom-call(s32[24]{0:T(128)S(1)} %collective-permute-done.req, s32[63]{0:T(128)S(1)} %get-tuple-element.72.pos, bf16[63,128,128]{2,1,0:T(8,128)(2,1)S(1)} %bitcast.17, bf16[9,128,128]{2,1,0:T(8,128)(2,1)S(1)} %collective-permute-done.3.rest_0_, ...), custom_call_target="tpu_custom_call" | custom-call | tf_op jit(solution)/shard_map/pick_right/pallas_call | solution.py:263
  52.4 2.5 %collective-permute-start.7 = (bf16[24,128,128]{2,1,0:T(8,128)(2,1)S(1)}, bf16[24,128,128]{2,1,0:T(8,128)(2,1)S(1)}, u32[]{:S(2)}, u32[]{:S(2)}) collective-permute-start(bf16[24,128,128]{2,1,0:T(8,128)(2,1)S(1)} %pick_right.1), channel_id=1, source_target_pairs={{0,24},{8,0},{16,8},{24,16},{1,25},{9,1},{17,9},{25,17},{2,26},{10... | collective-permute-start | bytes 2359304 | tf_op jit(solution)/shard_map/ppermute | solution.py:38
  54.8 5.8 %collective-permute-done.8.rest_5_.rest_6_ = bf16[9,128,128]{2,1,0:T(8,128)(2,1)} collective-permute-done((bf16[9,128,128]{2,1,0:T(8,128)(2,1)}, bf16[9,128,128]{2,1,0:T(8,128)(2,1)}, u32[]{:S(2)}, u32[]{:S(2)}) %collective-permute-start.8) | collective-permute-done | bytes 294944 | tf_op jit(solution)/shard_map/ppermute | solution.py:38
  60.6 2.3 %pick_left.1 = bf16[24,128,128]{2,1,0:T(8,128)(2,1)S(1)} custom-call(s32[25]{0:T(128)S(1)} %copy-done.7, s32[63]{0:T(128)S(1)} %get-tuple-element.72.pos, bf16[63,128,128]{2,1,0:T(8,128)(2,1)S(1)} %bitcast.18, bf16[9,128,128]{2,1,0:T(8,128)(2,1)S(1)} %collective-permute-done.3.rest_0_, bf16[9,128,128]{2,1,0:T(8,128)(2,1)S(1)} %collective-permute-done.2.rest_1_, ...), custom_call_target="tpu_custom_call" | custom-call | tf_op jit(solution)/shard_map/pick_left/pallas_call | solution.py:263
  62.9 3.7 %collective-permute-start.10 = (bf16[24,128,128]{2,1,0:T(8,128)(2,1)S(1)}, bf16[24,128,128]{2,1,0:T(8,128)(2,1)S(1)}, u32[]{:S(2)}, u32[]{:S(2)}) collective-permute-start(bf16[24,128,128]{2,1,0:T(8,128)(2,1)S(1)} %pick_left.1), channel_id=1, source_target_pairs={{0,7},{1,0},{2,1},{3,2},{4,3},{5,4},{6,5},{7,6},{8,15},{9,8},{10,9... | collective-permute-start | bytes 2359304 | tf_op jit(solution)/shard_map/ppermute | solution.py:38
  66.6 2.5 %collective-permute-start.11 = (bf16[9,128,128]{2,1,0:T(8,128)(2,1)}, bf16[9,128,128]{2,1,0:T(8,128)(2,1)S(1)}, u32[]{:S(2)}, u32[]{:S(2)}) collective-permute-start(bf16[9,128,128]{2,1,0:T(8,128)(2,1)} %collective-permute-done.8.rest_5_.rest_6_), channel_id=1, source_target_pairs={{0,24},{8,0},{16,8},{24,16},{1,25},{9,1},{17,9},{25,17},{2,26},{10... | collective-permute-start | bytes 884744 | tf_op jit(solution)/shard_map/ppermute | solution.py:38
  69.1 0.5 collective-permute-start.9
  69.6 3.2 %collective-permute-done.7.rest_1_ = bf16[24,128,128]{2,1,0:T(8,128)(2,1)S(1)} collective-permute-done((bf16[24,128,128]{2,1,0:T(8,128)(2,1)S(1)}, bf16[24,128,128]{2,1,0:T(8,128)(2,1)S(1)}, u32[]{:S(2)}, u32[]{:S(2)}) %collective-permute-start.7) | collective-permute-done | bytes 786464 | tf_op jit(solution)/shard_map/ppermute | solution.py:38
  72.8 2.9 %own_section.1.acc = f32[33,128,128]{2,1,0:T(8,128)S(1)} custom-call(s32[384]{0:T(512)S(1)} %bitcast.22, s32[2]{0:T(128)S(1)} %bitcast.23, s32[63]{0:T(128)S(1)} %get-tuple-element.72.pos, bf16[63,128,128]{2,1,0:T(8,128)(2,1)S(1)} %bitcast.19, bf16[9,128,128]{2,1,0:T(8,128)(2,1)S(1)} %collective-permute-done.3.rest_0_, ...), custom_call_target="tpu_custom_call" | custom-call | bytes 35000 | tf_op jit(solution)/shard_map/own_section/pallas_call | solution.py:324
  75.7 2.7 %collective-permute-done.9.pos_r = s32[63]{0:T(128)S(1)} collective-permute-done((s32[63]{0:T(128)S(1)}, s32[63]{0:T(128)S(1)}, u32[]{:S(2)}, u32[]{:S(2)}) %collective-permute-start.9) | collective-permute-done | bytes 284 | tf_op jit(solution)/shard_map/ppermute | solution.py:38
  78.5 4.2 %next_section.1 = bf16[32,128,128]{2,1,0:T(8,128)(2,1)} custom-call(s32[1]{0:T(128)} %bitcast.4.col.token, s32[384]{0:T(512)S(1)} %bitcast.21, s32[2]{0:T(128)S(1)} %bitcast.24, s32[128]{0:T(128)S(1)} %copy-done.5, s32[128]{0:T(128)S(1)} %copy-done.6, s32[63]{0:T(128)S(1)} %get-tuple-element.72.pos, s32[63]{0:T(128)S(1)} %collective-permute-done.9.pos_r, ...), custom_call_target="tpu_custom_call" | custom-call | bytes 35000 | tf_op jit(solution)/shard_map/next_section/pallas_call | solution.py:380
  (23 shorter events, 0.1 us)
Async XLA Ops:
  0.0 19.8 %copy-start.9 = (s32[1,1,2,128,3]{3,2,4,1,0:T(2,128)S(1)}, s32[1,1,2,128,3]{3,2,4,1,0:T(2,128)}, u32[]{:S(2)}) copy-start(s32[1,1,2,128,3]{3,2,4,1,0:T(2,128)} %param.6) | copy-start | bytes 9220
  3.1 16.1 %collective-permute-start.3 = (bf16[9,128,128]{2,1,0:T(8,128)(2,1)}, bf16[9,128,128]{2,1,0:T(8,128)(2,1)S(1)}, u32[]{:S(2)}, u32[]{:S(2)}) collective-permute-start(bf16[9,128,128]{2,1,0:T(8,128)(2,1)} %get-tuple-element.66), channel_id=1, source_target_pairs={{0,2},{1,3},{2,4},{3,5},{4,6},{5,7},{6,0},{7,1},{8,10},{9,11},{10,... | collective-permute-start | bytes 884744 | tf_op jit(solution)/shard_map/ppermute | solution.py:38
  6.2 16.8 %collective-permute-start.2 = (bf16[9,128,128]{2,1,0:T(8,128)(2,1)}, bf16[9,128,128]{2,1,0:T(8,128)(2,1)S(1)}, u32[]{:S(2)}, u32[]{:S(2)}) collective-permute-start(bf16[9,128,128]{2,1,0:T(8,128)(2,1)} %get-tuple-element.65), channel_id=1, source_target_pairs={{0,6},{1,7},{2,0},{3,1},{4,2},{5,3},{6,4},{7,5},{8,14},{9,15},{10,... | collective-permute-start | bytes 884744 | tf_op jit(solution)/shard_map/ppermute | solution.py:38
  8.9 1.6 %copy-start = (bf16[1,1,63,128,128]{4,3,2,1,0:T(8,128)(2,1)S(1)}, bf16[1,1,63,128,128]{4,3,2,1,0:T(8,128)(2,1)}, u32[]{:S(2)}) copy-start(bf16[1,1,63,128,128]{4,3,2,1,0:T(8,128)(2,1)} %param.4) | copy-start | bytes 6193156
  10.5 0.7 copy-start.4
  11.2 38.8 %copy-start.1 = (bf16[1,1,63,128,128]{4,3,2,1,0:T(8,128)(2,1)S(1)}, bf16[1,1,63,128,128]{4,3,2,1,0:T(8,128)(2,1)}, u32[]{:S(2)}) copy-start(bf16[1,1,63,128,128]{4,3,2,1,0:T(8,128)(2,1)} %param.4) | copy-start | bytes 6193156
  15.0 0.7 copy-start.8
  15.7 10.9 %collective-permute-start.1 = (bf16[9,128,128]{2,1,0:T(8,128)(2,1)}, bf16[9,128,128]{2,1,0:T(8,128)(2,1)S(1)}, u32[]{:S(2)}, u32[]{:S(2)}) collective-permute-start(bf16[9,128,128]{2,1,0:T(8,128)(2,1)} %get-tuple-element.64), channel_id=1, source_target_pairs={{0,7},{1,0},{2,1},{3,2},{4,3},{5,4},{6,5},{7,6},{8,15},{9,8},{10,9... | collective-permute-start | bytes 884744 | tf_op jit(solution)/shard_map/ppermute | solution.py:38
  16.6 16.7 %collective-permute-start.4 = (bf16[9,128,128]{2,1,0:T(8,128)(2,1)}, bf16[9,128,128]{2,1,0:T(8,128)(2,1)S(1)}, u32[]{:S(2)}, u32[]{:S(2)}) collective-permute-start(bf16[9,128,128]{2,1,0:T(8,128)(2,1)} %get-tuple-element.76), channel_id=1, source_target_pairs={{0,3},{1,4},{2,5},{3,6},{4,7},{5,0},{6,1},{7,2},{8,11},{9,12},{10,... | collective-permute-start | bytes 884744 | tf_op jit(solution)/shard_map/ppermute | solution.py:38
  16.6 21.9 %collective-permute-start.5 = (bf16[9,128,128]{2,1,0:T(8,128)(2,1)}, bf16[9,128,128]{2,1,0:T(8,128)(2,1)S(1)}, u32[]{:S(2)}, u32[]{:S(2)}) collective-permute-start(bf16[9,128,128]{2,1,0:T(8,128)(2,1)} %get-tuple-element.79), channel_id=1, source_target_pairs={{0,5},{1,6},{2,7},{3,0},{4,1},{5,2},{6,3},{7,4},{8,13},{9,14},{10,... | collective-permute-start | bytes 884744 | tf_op jit(solution)/shard_map/ppermute | solution.py:38
  19.2 27.8 %collective-permute-start.6 = (bf16[10,128,128]{2,1,0:T(8,128)(2,1)}, bf16[10,128,128]{2,1,0:T(8,128)(2,1)}, u32[]{:S(2)}, u32[]{:S(2)}) collective-permute-start(bf16[10,128,128]{2,1,0:T(8,128)(2,1)} %get-tuple-element.82.self_ref), channel_id=1, source_target_pairs={{0,1},{1,2},{2,3},{3,4},{4,5},{5,6},{6,7},{7,0},{8,9},{9,10},{10,1... | collective-permute-start | bytes 983048 | tf_op jit(solution)/shard_map/ppermute | solution.py:38
  23.0 4.5 %collective-permute-start = (s32[24]{0:T(128)}, s32[24]{0:T(128)S(1)}, u32[]{:S(2)}, u32[]{:S(2)}) collective-permute-start(s32[24]{0:T(128)} %get-tuple-element.62), channel_id=1, source_target_pairs={{0,8},{8,16},{16,24},{24,0},{1,9},{9,17},{17,25},{25,1},{2,10},{10... | collective-permute-start | bytes 296 | tf_op jit(solution)/shard_map/ppermute | solution.py:38
  38.4 22.2 %collective-permute-start.8 = (bf16[9,128,128]{2,1,0:T(8,128)(2,1)}, bf16[9,128,128]{2,1,0:T(8,128)(2,1)}, u32[]{:S(2)}, u32[]{:S(2)}) collective-permute-start(bf16[9,128,128]{2,1,0:T(8,128)(2,1)} %copy-done.8), channel_id=1, source_target_pairs={{0,4},{1,5},{2,6},{3,7},{4,0},{5,1},{6,2},{7,3},{8,12},{9,13},{10,... | collective-permute-start | bytes 884744 | tf_op jit(solution)/shard_map/ppermute | solution.py:38
  50.0 10.6 %copy-start.7 = (s32[25]{0:T(128)S(1)}, s32[25]{0:T(128)}, u32[]{:S(2)}) copy-start(s32[25]{0:T(128)} %asked.1.req) | copy-start | bytes 304
  52.3 20.4 %copy-start.3 = (s32[1,1,2]{2,1,0:T(1,128)S(1)}, s32[1,1,2]{2,1,0:T(1,128)}, u32[]{:S(2)}) copy-start(s32[1,1,2]{2,1,0:T(1,128)} %param.7) | copy-start | bytes 28
  52.4 20.4 %collective-permute-start.7 = (bf16[24,128,128]{2,1,0:T(8,128)(2,1)S(1)}, bf16[24,128,128]{2,1,0:T(8,128)(2,1)S(1)}, u32[]{:S(2)}, u32[]{:S(2)}) collective-permute-start(bf16[24,128,128]{2,1,0:T(8,128)(2,1)S(1)} %pick_right.1), channel_id=1, source_target_pairs={{0,24},{8,0},{16,8},{24,16},{1,25},{9,1},{17,9},{25,17},{2,26},{10... | collective-permute-start | bytes 2359304 | tf_op jit(solution)/shard_map/ppermute | solution.py:38
  62.9 15.5 %collective-permute-start.10 = (bf16[24,128,128]{2,1,0:T(8,128)(2,1)S(1)}, bf16[24,128,128]{2,1,0:T(8,128)(2,1)S(1)}, u32[]{:S(2)}, u32[]{:S(2)}) collective-permute-start(bf16[24,128,128]{2,1,0:T(8,128)(2,1)S(1)} %pick_left.1), channel_id=1, source_target_pairs={{0,7},{1,0},{2,1},{3,2},{4,3},{5,4},{6,5},{7,6},{8,15},{9,8},{10,9... | collective-permute-start | bytes 2359304 | tf_op jit(solution)/shard_map/ppermute | solution.py:38
  66.6 11.8 %collective-permute-start.11 = (bf16[9,128,128]{2,1,0:T(8,128)(2,1)}, bf16[9,128,128]{2,1,0:T(8,128)(2,1)S(1)}, u32[]{:S(2)}, u32[]{:S(2)}) collective-permute-start(bf16[9,128,128]{2,1,0:T(8,128)(2,1)} %collective-permute-done.8.rest_5_.rest_6_), channel_id=1, source_target_pairs={{0,24},{8,0},{16,8},{24,16},{1,25},{9,1},{17,9},{25,17},{2,26},{10... | collective-permute-start | bytes 884744 | tf_op jit(solution)/shard_map/ppermute | solution.py:38
  69.1 9.3 %collective-permute-start.9 = (s32[63]{0:T(128)S(1)}, s32[63]{0:T(128)S(1)}, u32[]{:S(2)}, u32[]{:S(2)}) collective-permute-start(s32[63]{0:T(128)S(1)} %get-tuple-element.72.pos), channel_id=1, source_target_pairs={{0,24},{8,0},{16,8},{24,16},{1,25},{9,1},{17,9},{25,17},{2,26},{10... | collective-permute-start | bytes 764 | tf_op jit(solution)/shard_map/ppermute | solution.py:38
  72.8 5.6 %copy-start.2 = (s32[3,128]{1,0:T(4,128)S(1)}, s32[3,128]{1,0:T(4,128)}, u32[]{:S(2)}) copy-start(s32[3,128]{1,0:T(4,128)} %get-tuple-element.107) | copy-start | bytes 4612
  72.8 5.6 %copy-start.5 = (s32[128]{0:T(128)S(1)}, s32[128]{0:T(128)}, u32[]{:S(2)}) copy-start(s32[128]{0:T(128)} %get-tuple-element.102.slots_l) | copy-start | bytes 1540
  72.8 5.7 %copy-start.6 = (s32[128]{0:T(128)S(1)}, s32[128]{0:T(128)}, u32[]{:S(2)}) copy-start(s32[128]{0:T(128)} %get-tuple-element.103.slots_r) | copy-start | bytes 1540

commit v3 on v2

--- a/solution.py
+++ b/solution.py
@@ -9,8 +9,9 @@
 
 OUTSLOTS = 32
 USED = 24
-UNROLL = 8
-FIRST = 2
+UNROLL = 16
+NEXT_UNROLL = 16
+FIRST = 1
 LEFT_PIECES = 1
 RIGHT_PIECES = 1
 FIRST_MIB = 62
@@ -62,7 +63,8 @@
         others = others[1:3] + others[:1] + others[3:]
         pieces = min(5, len(others))
         cuts = [len(others) * i // pieces for i in range(pieces + 1)]
-        self.stages = [others[a:b] for a, b in zip(cuts, cuts[1:])] + [[1], [half]]
+        groups = [others[a:b] for a, b in zip(cuts, cuts[1:])]
+        self.stages = groups[:3] + [[1]] + groups[3:] + [[half]]
         self.base = [0] * cols
         self.start = []
         at = 0
@@ -123,7 +125,7 @@
     )(targets, col, stored)
 
 
-def rest_kernel(lay, tgt, col, ids, stored_ref, *rest):
+def rest_kernel(lay, tgt, col, plan, stored_ref, *rest):
     outs, pos, inv, cnt = rest[:-3], rest[-3], rest[-2], rest[-1]
     for d in range(lay.cols):
         cnt[d] = lay.base[d]
@@ -143,15 +145,15 @@
             outs[s - FIRST][j] = stored_ref[inv[lay.start[s] + j]].T
             return carry
 
-        lax.fori_loop(0, lay.size(s), flip, 0, unroll=lay.size(s) % 3 == 0 and 3 or 1)
+        lax.fori_loop(0, lay.size(s), flip, 0, unroll=9 if lay.size(s) % 9 == 0 else 1)
     note = outs[lay.self_stage - FIRST]
-    rows, block = ids.shape
-    for row in range(rows):
-        line = ids[row : row + 1, :].astype(jnp.float32)
+    block = note.shape[-1]
+    for row in range(plan.shape[2] // block):
+        line = plan[0, 1:2, row * block : row * block + block].astype(jnp.float32)
         note[lay.size(lay.self_stage), row * 16 : row * 16 + 16, :] = jnp.broadcast_to(line, (16, block)).astype(note.dtype)
 
 
-def rest_stages(lay, targets, col, ids, stored):
+def rest_stages(lay, targets, col, plan, stored):
     block = stored.shape[-1]
     shapes = tuple(
         jax.ShapeDtypeStruct((lay.size(s) + (s == lay.self_stage), block, block), stored.dtype)
@@ -166,7 +168,7 @@
         compiler_params=params(12),
         cost_estimate=cost(0.01),
         name="rest_stages",
-    )(targets, col, ids, stored)
+    )(targets, col, plan, stored)
 
 
 def wanted_kernel(prods, plan, reqs_r, slots_l, slots_r, seen_l, seen_r):
@@ -181,7 +183,7 @@
 
     def step(p, counts):
         sides = ((slots_l, seen_l), (slots_r, seen_r))
-        found = [plan[side * prods + p] for side in range(2)]
+        found = [plan[side, 1, p] for side in range(2)]
         known = [seen[which] for (_, seen), which in zip(sides, found)]
         slot = [jnp.where(k < 0, n, k) for k, n in zip(known, counts)]
         for (slots, seen), which, at in zip(sides, found, slot):
@@ -193,7 +195,7 @@
     lax.fori_loop(0, prods, step, (jnp.int32(0), jnp.int32(0)), unroll=4)
 
 
-def wanted(panel_size, plan_flat, prods):
+def wanted(panel_size, plan, prods):
     return pl.pallas_call(
         functools.partial(wanted_kernel, prods),
         out_shape=(i32(USED), i32(prods), i32(prods)),
@@ -202,7 +204,7 @@
         scratch_shapes=[pltpu.SMEM((panel_size,), jnp.int32)] * 2,
         cost_estimate=cost(0.01),
         name="wanted",
-    )(plan_flat)
+    )(plan)
 
 
 def asked_kernel(ids, reqs, seen):
@@ -237,25 +239,15 @@
     parts, outs = rest[: len(stages)], rest[len(stages) :]
     size = USED // pieces
     for piece, out in enumerate(outs):
-
-        def step(n, carry, piece=piece, out=out):
+        for n in range(size):
             which = req[piece * size + n]
             lower = which >= lay.stored
             q = pos[jnp.where(lower, which - lay.stored, 0)]
-
-            @pl.when(jnp.logical_not(lower))
-            def _():
-                out[n] = stored_ref[which]
-
+            value = stored_ref[jnp.where(lower, 0, which)]
             for s, part in zip(stages, parts):
-
-                @pl.when(lower & (q >= lay.start[s]) & (q < lay.start[s + 1]))
-                def _(s=s, part=part):
-                    out[n] = part[q - lay.start[s]]
-
-            return carry
-
-        lax.fori_loop(0, size, step, 0)
+                at = jnp.clip(q - lay.start[s], 0, lay.size(s) - 1)
+                value = jnp.where(lower & (q >= lay.start[s]), part[at], value)
+            out[n] = value
 
 
 def pick(lay, stages, pieces, req, pos, stored, parts, name):
@@ -313,14 +305,14 @@
         return jnp.where(lower, lay.stored + pos[jnp.where(lower, which - lay.stored, 0)], which)
 
     def entry(p):
-        return where(plan[p]), where(plan[prods + p]), plan[2 * prods + p]
+        return where(plan[0, 0, p]), where(plan[1, 0, p]), plan[2, 0, p]
 
     multiply(counts[0], entry, panel, panel, acc)
 
 
-def own_section(lay, plan_flat, counts, pos, stored, parts):
+def own_section(lay, plan, counts, pos, stored, parts):
     block = stored.shape[-1]
-    prods = plan_flat.shape[0] // 3
+    prods = plan.shape[2]
     return pl.pallas_call(
         functools.partial(own_kernel, lay, prods),
         out_shape=jax.ShapeDtypeStruct((OUTSLOTS + 1, block, block), jnp.float32),
@@ -333,64 +325,83 @@
         compiler_params=params(20),
         cost_estimate=cost(0.01),
         name="own_section",
-    )(plan_flat, counts, pos, stored, *parts)
-
-
-def next_kernel(lay, late, prods, token, plan, counts, slots_l, slots_r, pos, pos_r, acc, self_ref, *rest):
-    lefts, rights, parts = rest[:LEFT_PIECES], rest[LEFT_PIECES : LEFT_PIECES + RIGHT_PIECES], rest[LEFT_PIECES + RIGHT_PIECES : -4]
-    out, left, right, sem = rest[-4:]
-    late_from = lay.start[late[0]] if late else lay.total
-    moves = [(self_ref, left, USED, lay.size(lay.self_stage))]
-    moves += [(part, left, n * part.shape[0], part.shape[0]) for n, part in enumerate(lefts)]
-    moves += [(part, right, n * part.shape[0], part.shape[0]) for n, part in enumerate(rights)]
-    moves += [(part, right, USED + lay.start[s] - late_from, lay.size(s)) for s, part in zip(late, parts)]
-    copies = [
-        pltpu.make_async_copy(part.at[pl.ds(0, size)], whole.at[pl.ds(at, size)], sem.at[n])
-        for n, (part, whole, at, size) in enumerate(moves)
-    ]
-    for copy in copies:
-        copy.start()
-    for copy in copies:
-        copy.wait()
-
-    def where(which, slot, table, first, last):
-        lower = which >= lay.stored
-        q = table[jnp.where(lower, which - lay.stored, 0)]
-        return jnp.where(lower & (q >= first) & (q < last), USED + q - first, slot)
-
-    def entry(p):
-        own = lay.self_stage
-        i = where(plan[p], slots_l[p], pos, lay.start[own], lay.start[own + 1])
-        j = where(plan[prods + p], slots_r[p], pos_r, late_from, lay.total)
-        return i, j, plan[2 * prods + p]
-
-    multiply(counts[1], entry, left, right, acc)
-
-    def finish(o, carry):
+    )(plan, counts, pos, stored, *parts)
+
+
+def places_kernel(lay, late, plan, counts, slots_l, slots_r, pos, pos_r, out):
+    own_from, own_to = lay.start[lay.self_stage], lay.start[lay.self_stage + 1]
+    late_from = lay.start[late[0]]
+
+    def step(p, carry):
+        left_id, right_id = plan[0, 1, p], plan[1, 1, p]
+        lower = left_id >= lay.stored
+        q = pos[jnp.where(lower, left_id - lay.stored, 0)]
+        out[0, p] = jnp.where(lower & (q >= own_from) & (q < own_to), USED + q - own_from, slots_l[p])
+        lower = right_id >= lay.stored
+        q = pos_r[jnp.where(lower, right_id - lay.stored, 0)]
+        out[1, p] = jnp.where(lower & (q >= late_from), USED + q - late_from, slots_r[p])
+        out[2, p] = jnp.where(p < counts[1], plan[2, 1, p], OUTSLOTS)
+        return carry
+
+    lax.fori_loop(0, plan.shape[2], step, 0, unroll=4)
+
+
+def places(lay, late, plan, counts, slots_l, slots_r, pos, pos_r):
+    return pl.pallas_call(
+        functools.partial(places_kernel, lay, late),
+        out_shape=i32(3, plan.shape[2]),
+        in_specs=[SMEM] * 6,
+        out_specs=SMEM,
+        name="places",
+    )(plan, counts, slots_l, slots_r, pos, pos_r)
+
+
+def either(n, first, first_size, others):
+    value = first[jnp.minimum(n, first_size - 1)]
+    at = first_size
+    for part, size in others:
+        value = jnp.where(n >= at, part[jnp.clip(n - at, 0, size - 1)], value)
+        at += size
+    return value
+
+
+def next_kernel(lay, late, token, spots, counts, old, self_ref, left, right, *rest):
+    parts, (acc, out) = rest[:-2], rest[-2:]
+    lefts = [(self_ref, lay.size(lay.self_stage))]
+    rights = [(part, lay.size(s)) for s, part in zip(late, parts)]
+
+    def group(g, carry):
+        found = []
+        for u in range(NEXT_UNROLL):
+            p = g * NEXT_UNROLL + u
+            i, j, o = spots[0, p], spots[1, p], spots[2, p]
+            a = either(i, left, USED, lefts)
+            b = either(j, right, USED, rights)
+            found.append((o, jnp.dot(a, b, preferred_element_type=jnp.float32)))
+        for o, term in found:
+            acc[o] += term
+        return carry
+
+    lax.fori_loop(0, (counts[1] + NEXT_UNROLL - 1) // NEXT_UNROLL, group, 0)
+    for o in range(OUTSLOTS):
         out[o] = acc[o].astype(out.dtype)
-        return carry
-
-    lax.fori_loop(0, OUTSLOTS, finish, 0)
-
-
-def next_section(lay, late, token, plan_flat, counts, slots_l, slots_r, pos, pos_r, acc, left, self_part, right, parts):
+
+
+def next_section(lay, late, token, spots, counts, acc, self_part, left, right, parts):
     block = self_part.shape[-1]
-    prods = plan_flat.shape[0] // 3
-    late_size = sum(lay.size(s) for s in late)
-    return pl.pallas_call(
-        functools.partial(next_kernel, lay, late, prods),
-        out_shape=jax.ShapeDtypeStruct((OUTSLOTS, block, block), self_part.dtype),
-        in_specs=[SMEM] * 7 + [VMEM] * (2 + len(left) + len(right) + len(parts)),
-        out_specs=VMEM,
-        scratch_shapes=[
-            pltpu.VMEM((USED + lay.size(lay.self_stage), block, block), self_part.dtype),
-            pltpu.VMEM((USED + late_size, block, block), self_part.dtype),
-            pltpu.SemaphoreType.DMA((1 + len(left) + len(right) + len(parts),)),
-        ],
+    return pl.pallas_call(
+        functools.partial(next_kernel, lay, late),
+        out_shape=(
+            jax.ShapeDtypeStruct(acc.shape, acc.dtype),
+            jax.ShapeDtypeStruct((OUTSLOTS, block, block), self_part.dtype),
+        ),
+        in_specs=[SMEM] * 3 + [VMEM] * (4 + len(parts)),
+        out_specs=(VMEM, VMEM),
+        input_output_aliases={3: 0},
         compiler_params=params(20),
         cost_estimate=cost(0.01),
         name="next_section",
-    )(token, plan_flat, counts, slots_l, slots_r, pos, pos_r, acc, self_part, *left, *right, *parts)
+    )(token, spots, counts, acc, self_part, left, right, *parts)[1]
 
 
 FLIGHT = 2
@@ -401,9 +412,8 @@
     stored = upper_blocks[0, 0]
     targets = block_targets[0, 0]
     counts = live_counts[0, 0]
-    plan = jnp.swapaxes(product_plan[0, 0], 1, 2)
+    plan = jnp.transpose(product_plan[0, 0], (2, 0, 1))
     prods = plan.shape[2]
-    plans = plan.reshape(2, 3 * prods)
     lay = Layout(stored.shape[0], lax.axis_size("col"))
     stages = list(range(len(lay.stages)))
     early, late = stages[:EARLY], stages[EARLY:]
@@ -418,25 +428,26 @@
         return jnp.concatenate(parts, axis=0)
 
     order = Order(col)
-    sends = list(first_stage(lay, targets, col, stored))
+    sends = list(order.gate(first_stage(lay, targets, col, stored)))
     got = [exchange(s, sends[s]) for s in range(FIRST)]
-    *rest, pos = rest_stages(lay, targets, col, plans[1, :prods].reshape(-1, stored.shape[-1]), order.gate(stored))
+    *rest, pos = rest_stages(lay, targets, col, plan, order.gate(stored))
     sends += rest
-    got += [exchange(s, sends[s]) for s in stages[FIRST:4]]
-    reqs_r, slots_l, slots_r = order.gate(wanted(2 * lay.stored, order.gate(plans[1]), prods))
+    got += [exchange(s, sends[s]) for s in stages[FIRST:-1]]
+    for s in stages[:2]:
+        got[s] = order.gate(got[s])
+    reqs_r, slots_l, slots_r = order.gate(wanted(2 * lay.stored, order.gate(plan), prods))
     asked_r = moved(reqs_r, "row", 1)
     pos_r = moved(pos, "row", -1)
-    got += [exchange(s, sends[s]) for s in stages[4:-1]]
-    for s in stages[:3]:
-        got[s] = order.gate(got[s])
-    asked_r = order.gate(asked_r)
-    for s in stages[3:-2]:
-        got[s] = order.gate(got[s])
-    got.append(exchange(stages[-1], order.gate(sends[-1])))
-    got[-2] = order.gate(got[-2])
+    got[2] = order.gate(got[2])
+    got[3] = order.gate(got[3])
+    asked_r, pos_r = order.gate((asked_r, pos_r))
     rows = prods // stored.shape[-1]
     ids = got[lay.self_stage][-1, : 16 * rows : 16].reshape(-1).astype(jnp.int32)
     asked_l = order.gate(asked(2 * lay.stored, order.gate(ids)))
+    spots = order.gate(places(lay, late, plan, counts, slots_l, slots_r, pos, pos_r))
+    for s in stages[4:-1]:
+        got[s] = order.gate(got[s])
+    got.append(exchange(stages[-1], order.gate(sends[-1])))
     picked = order.gate(pick(lay, early, RIGHT_PIECES, asked_r, pos, stored, [got[s] for s in early], "pick_right"))
     right = [moved(piece, "row", -1) for piece in picked]
     got[-1] = order.gate(got[-1])
@@ -444,11 +455,8 @@
     ready = [s for s in stages if s != lay.self_stage]
     picked = pick(lay, ready, LEFT_PIECES, order.gate(asked_l), pos, stored, [got[s] for s in ready], "pick_left")
     left = [moved(piece, "col", -1) for piece in order.gate(picked)]
-    right = order.gate(right)
-    acc = own_section(lay, order.gate(plans[0]), counts, pos, stored, got)
-    out = next_section(
-        lay, late, order.token, plans[1], counts, slots_l, slots_r, pos, pos_r, acc, left, sends[lay.self_stage], right, forwarded
-    )
+    acc = own_section(lay, plan, counts, pos, stored, got)
+    out = next_section(lay, late, order.token, spots, counts, acc, sends[lay.self_stage], *left, *right, forwarded)
     return out[None, None]
 
 

time: 82.9 us -> 80 us (0.965)
  the two profiles are of different devices: /device:TPU:0 before, /device:TPU:31 now
where the time goes in v3:
time: 80 us; the launch traced here: 79.8 us
  waiting for transfers between devices  38.7 us (48%)
  Pallas kernels  24.8 us (31%)
  starting transfers between devices  12.7 us (16%)
  local copies, waits for them, and re-layouts  2.2 us (3%)
  other arithmetic  1.17 us (1%)
    ppermute x12, waiting for transfers between devices, moved(): lax.ppermute(value, axis, [(s, (s + steps) % count) for s in range(count)])  38.7 us
    ppermute x12, starting transfers between devices, moved(): lax.ppermute(value, axis, [(s, (s + steps) % count) for s in range(count)])  12.7 us
    pallas_call x1, Pallas kernels, next_section(): pl.pallas_call(functools.partial(next_kernel, lay, late), out_shape=(jax....  4.51 us
    pallas_call x1, Pallas kernels, own_section(): pl.pallas_call(functools.partial(own_kernel, lay, prods), out_shape=jax.S...  4.07 us
    pallas_call x2, Pallas kernels, pick(): pl.pallas_call(functools.partial(pick_kernel, lay, stages, pieces), out_s...  3 us
    pallas_call x1, Pallas kernels, places(): pl.pallas_call(functools.partial(places_kernel, lay, late), out_shape=i32...  2.94 us
    pallas_call x1, Pallas kernels, rest_stages(): pl.pallas_call(functools.partial(rest_kernel, lay), out_shape=shapes + (i...  2.91 us
    pallas_call x1, Pallas kernels, wanted(): pl.pallas_call(functools.partial(wanted_kernel, prods), out_shape=(i32(US...  2.85 us
  transfers between devices with their start and end apart: 12, of which 5 were waited for; matrix products, arithmetic and copies ran while one was open for 1% of the time, Pallas kernels for 22%

profile of v3, /device:TPU:31, one launch (start us, length us, event | category | flops | bytes accessed | tf_op | source)
XLA Modules:
  0.0 79.8 jit_solution(7160193519394542978)
XLA Ops:
  0.0 2.7 %first_stage.1 = bf16[9,128,128]{2,1,0:T(8,128)(2,1)} custom-call(s32[63]{0:T(128)} %bitcast.23, s32[1]{0:T(128)} %bitcast.1.col.token, bf16[63,128,128]{2,1,0:T(8,128)(2,1)} %bitcast.11), custom_call_target="tpu_custom_call" | custom-call | tf_op jit(solution)/shard_map/first_stage/pallas_call | solution.py:113
  2.7 0.1 collective-permute-start.3
  2.8 0.0 copy-start
  2.8 1.6 %copy-done = bf16[1,1,63,128,128]{4,3,2,1,0:T(8,128)(2,1)S(1)} copy-done((bf16[1,1,63,128,128]{4,3,2,1,0:T(8,128)(2,1)S(1)}, bf16[1,1,63,128,128]{4,3,2,1,0:T(8,128)(2,1)}, u32[]{:S(2)}) %copy-start) | copy-done | bytes 2064408
  4.4 2.9 %rest_stages.1 = (bf16[9,128,128]{2,1,0:T(8,128)(2,1)S(1)}, bf16[9,128,128]{2,1,0:T(8,128)(2,1)}, bf16[10,128,128]{2,1,0:T(8,128)(2,1)}, bf16[9,128,128]{2,1,0:T...) custom-call(s32[63]{0:T(128)S(1)} %bitcast.24, s32[1]{0:T(128)} %bitcast.1.col.token, ...), custom_call_target="tpu_custom_call" | custom-call | bytes 35000 | tf_op jit(solution)/shard_map/rest_stages/pallas_call | solution.py:162
  7.3 2.1 %collective-permute-start = (bf16[10,128,128]{2,1,0:T(8,128)(2,1)}, bf16[10,128,128]{2,1,0:T(8,128)(2,1)}, u32[]{:S(2)}, u32[]{:S(2)}) collective-permute-start(bf16[10,128,128]{2,1,0:T(8,128)(2,1)} %get-tuple-element.59.self_ref), channel_id=1, source_target_pairs={{0,1},{1,2},{2,3},{3,4},{4,5},{5,6},{6,7},{7,0},{8,9},{9,10},{10,1... | collective-permute-start | bytes 983048 | tf_op jit(solution)/shard_map/ppermute | solution.py:39
  9.5 0.2 collective-permute-start.2
  9.6 1.1 %collective-permute-start.1 = (bf16[9,128,128]{2,1,0:T(8,128)(2,1)}, bf16[9,128,128]{2,1,0:T(8,128)(2,1)S(1)}, u32[]{:S(2)}, u32[]{:S(2)}) collective-permute-start(bf16[9,128,128]{2,1,0:T(8,128)(2,1)} %get-tuple-element.60), channel_id=1, source_target_pairs={{0,7},{1,0},{2,1},{3,2},{4,3},{5,4},{6,5},{7,6},{8,15},{9,8},{10,9... | collective-permute-start | bytes 884744 | tf_op jit(solution)/shard_map/ppermute | solution.py:39
  10.7 2.6 %collective-permute-start.7 = (bf16[9,128,128]{2,1,0:T(8,128)(2,1)}, bf16[9,128,128]{2,1,0:T(8,128)(2,1)S(1)}, u32[]{:S(2)}, u32[]{:S(2)}) collective-permute-start(bf16[9,128,128]{2,1,0:T(8,128)(2,1)} %get-tuple-element.83), channel_id=1, source_target_pairs={{0,3},{1,4},{2,5},{3,6},{4,7},{5,0},{6,1},{7,2},{8,11},{9,12},{10,... | collective-permute-start | bytes 884744 | tf_op jit(solution)/shard_map/ppermute | solution.py:39
  13.3 10.4 %collective-permute-done.2.rest_1_ = bf16[9,128,128]{2,1,0:T(8,128)(2,1)S(1)} collective-permute-done((bf16[9,128,128]{2,1,0:T(8,128)(2,1)S(1)}, bf16[9,128,128]{2,1,0:T(8,128)(2,1)S(1)}, u32[]{:S(2)}, u32[]{:S(2)}) %collective-permute-start.2) | collective-permute-done | bytes 294944 | tf_op jit(solution)/shard_map/ppermute | solution.py:39
  23.7 0.3 collective-permute-start.5
  23.9 2.8 %wanted.1 = (s32[24]{0:T(128)}, s32[128]{0:T(128)}, s32[128]{0:T(128)}) custom-call(s32[3,2,128]{2,1,0:T(2,128)} %bitcast.16), custom_call_target="tpu_custom_call" | custom-call | bytes 35000 | tf_op jit(solution)/shard_map/wanted/pallas_call | solution.py:199
  26.8 2.2 %collective-permute-start.4 = (s32[24]{0:T(128)}, s32[24]{0:T(128)S(1)}, u32[]{:S(2)}, u32[]{:S(2)}) collective-permute-start(s32[24]{0:T(128)} %get-tuple-element.74), channel_id=1, source_target_pairs={{0,8},{8,16},{16,24},{24,0},{1,9},{9,17},{17,25},{25,1},{2,10},{10... | collective-permute-start | bytes 296 | tf_op jit(solution)/shard_map/ppermute | solution.py:39
  29.0 0.9 %collective-permute-done.4.req = s32[24]{0:T(128)S(1)} collective-permute-done((s32[24]{0:T(128)}, s32[24]{0:T(128)S(1)}, u32[]{:S(2)}, u32[]{:S(2)}) %collective-permute-start.4) | collective-permute-done | bytes 128 | tf_op jit(solution)/shard_map/ppermute | solution.py:39
  29.9 1.2 %bitcast_convert_fusion.ids = s32[128]{0:T(128)} fusion(bf16[10,128,128]{2,1,0:T(8,128)(2,1)} %collective-permute-done.rest_3_), kind=kLoop, calls=%fused_computation | loop fusion | flops 128 | bytes 768 | tf_op jit(solution)/shard_map/convert_element_type | solution.py:445
  31.0 1.8 %asked.1.req = s32[25]{0:T(128)} custom-call(s32[128]{0:T(128)} %bitcast_convert_fusion.ids), custom_call_target="tpu_custom_call" | custom-call | tf_op jit(solution)/shard_map/asked/pallas_call | solution.py:228
  32.9 2.9 %places.1.spots = s32[3,128]{1,0:T(4,128)} custom-call(s32[3,2,128]{2,1,0:T(2,128)} %bitcast.17, s32[2]{0:T(128)} %bitcast.20, s32[128]{0:T(128)} %get-tuple-element.84.slots_l, s32[128]{0:T(128)} %get-tuple-element.85.slots_r, s32[63]{0:T(128)} %copy-done.5, s32[63]{0:T(128)} %copy-done.12), custom_call_target="tpu_custom_call" | custom-call | tf_op jit(solution)/shard_map/places/pallas_call | solution.py:350
  35.8 8.1 %collective-permute-done.6.rest_5_.rest_4_ = bf16[9,128,128]{2,1,0:T(8,128)(2,1)S(1)} collective-permute-done((bf16[9,128,128]{2,1,0:T(8,128)(2,1)}, bf16[9,128,128]{2,1,0:T(8,128)(2,1)S(1)}, u32[]{:S(2)}, u32[]{:S(2)}) %collective-permute-start.6) | collective-permute-done | bytes 294944 | tf_op jit(solution)/shard_map/ppermute | solution.py:39
  44.0 2.6 %collective-permute-start.8 = (bf16[9,128,128]{2,1,0:T(8,128)(2,1)}, bf16[9,128,128]{2,1,0:T(8,128)(2,1)S(1)}, u32[]{:S(2)}, u32[]{:S(2)}) collective-permute-start(bf16[9,128,128]{2,1,0:T(8,128)(2,1)} %copy-done.11), channel_id=1, source_target_pairs={{0,4},{1,5},{2,6},{3,7},{4,0},{5,1},{6,2},{7,3},{8,12},{9,13},{10,... | collective-permute-start | bytes 884744 | tf_op jit(solution)/shard_map/ppermute | solution.py:39
  46.6 0.6 copy-done.6
  47.2 1.7 %pick_right.1 = bf16[24,128,128]{2,1,0:T(8,128)(2,1)S(1)} custom-call(s32[24]{0:T(128)S(1)} %collective-permute-done.4.req, s32[63]{0:T(128)S(1)} %copy-done.6, bf16[63,128,128]{2,1,0:T(8,128)(2,1)S(1)} %bitcast.13, bf16[9,128,128]{2,1,0:T(8,128)(2,1)S(1)} %collective-permute-done.3.rest_0_, bf16[9,128,128]{2,1,0:T(8,128)(2,1)S(1)} %collective-permute-done.2.rest_1_, ...), custom_call_target="tpu_custom_call" | custom-call | tf_op jit(solution)/shard_map/pick_right/pallas_call | solution.py:255
  48.9 0.0 copy-start.3
  48.9 0.0 copy-start.8
  48.9 1.1 %collective-permute-start.10 = (bf16[24,128,128]{2,1,0:T(8,128)(2,1)S(1)}, bf16[24,128,128]{2,1,0:T(8,128)(2,1)S(1)}, u32[]{:S(2)}, u32[]{:S(2)}) collective-permute-start(bf16[24,128,128]{2,1,0:T(8,128)(2,1)S(1)} %pick_right.1), channel_id=1, source_target_pairs={{0,24},{8,0},{16,8},{24,16},{1,25},{9,1},{17,9},{25,17},{2,26},{10... | collective-permute-start | bytes 2359304 | tf_op jit(solution)/shard_map/ppermute | solution.py:39
  50.1 9.8 %collective-permute-done.8.rest_5_.rest_6_ = bf16[9,128,128]{2,1,0:T(8,128)(2,1)S(1)} collective-permute-done((bf16[9,128,128]{2,1,0:T(8,128)(2,1)}, bf16[9,128,128]{2,1,0:T(8,128)(2,1)S(1)}, u32[]{:S(2)}, u32[]{:S(2)}) %collective-permute-start.8) | collective-permute-done | bytes 294944 | tf_op jit(solution)/shard_map/ppermute | solution.py:39
  59.9 1.3 %pick_left.1 = bf16[24,128,128]{2,1,0:T(8,128)(2,1)S(1)} custom-call(s32[25]{0:T(128)S(1)} %copy-done.10, s32[63]{0:T(128)S(1)} %copy-done.6, bf16[63,128,128]{2,1,0:T(8,128)(2,1)S(1)} %bitcast.14, bf16[9,128,128]{2,1,0:T(8,128)(2,1)S(1)} %collective-permute-done.3.rest_0_, bf16[9,128,128]{2,1,0:T(8,128)(2,1)S(1)} %collective-permute-done.2.rest_1_, ...), custom_call_target="tpu_custom_call" | custom-call | tf_op jit(solution)/shard_map/pick_left/pallas_call | solution.py:255
  61.2 0.0 copy-start.4
  61.2 0.3 collective-permute-start.9
  61.5 0.3 collective-permute-start.11
  61.8 4.1 %own_section.1.old = f32[33,128,128]{2,1,0:T(8,128)S(1)} custom-call(s32[3,2,128]{2,1,0:T(2,128)S(1)} %bitcast.19, s32[2]{0:T(128)S(1)} %bitcast.21, s32[63]{0:T(128)S(1)} %copy-done.7, bf16[63,128,128]{2,1,0:T(8,128)(2,1)S(1)} %bitcast.15, bf16[9,128,128]{2,1,0:T(8,128)(2,1)S(1)} %collective-permute-done.3.rest_0_, ...), custom_call_target="tpu_custom_call" | custom-call | bytes 35000 | tf_op jit(solution)/shard_map/own_section/pallas_call | solution.py:316
  65.9 9.4 %collective-permute-done.11.rest_0_ = bf16[9,128,128]{2,1,0:T(8,128)(2,1)S(1)} collective-permute-done((bf16[9,128,128]{2,1,0:T(8,128)(2,1)S(1)}, bf16[9,128,128]{2,1,0:T(8,128)(2,1)S(1)}, u32[]{:S(2)}, u32[]{:S(2)}) %collective-permute-start.11) | collective-permute-done | bytes 294944 | tf_op jit(solution)/shard_map/ppermute | solution.py:39
  75.3 4.5 %next_section.1 = (f32[33,128,128]{2,1,0:T(8,128)S(1)}, bf16[32,128,128]{2,1,0:T(8,128)(2,1)}) custom-call(s32[1]{0:T(128)} %bitcast.1.col.token, s32[3,128]{1,0:T(4,128)S(1)} %copy-done.4, s32[2]{0:T(128)S(1)} %bitcast.22, f32[33,128,128]{2,1,0:T(8,128)S(1)} %own_section.1.old, ...), custom_call_target="tpu_custom_call", output_to_operand_aliasing={{0}: (3, {})} | custom-call | bytes 35000 | tf_op jit(solution)/shard_map/next_section/pallas_call | solution.py:392
  (28 shorter events, 0.1 us)
Async XLA Ops:
  0.0 2.8 %copy-start.9 = (s32[1,1,63]{2,1,0:T(1,128)S(1)}, s32[1,1,63]{2,1,0:T(1,128)}, u32[]{:S(2)}) copy-start(s32[1,1,63]{2,1,0:T(1,128)} %param.5) | copy-start | bytes 760
  0.0 2.8 %copy-start.2 = (s32[1,1,2,128,3]{3,2,4,1,0:T(2,128)S(1)}, s32[1,1,2,128,3]{3,2,4,1,0:T(2,128)}, u32[]{:S(2)}) copy-start(s32[1,1,2,128,3]{3,2,4,1,0:T(2,128)} %param.6) | copy-start | bytes 9220
  2.7 10.5 %collective-permute-start.3 = (bf16[9,128,128]{2,1,0:T(8,128)(2,1)}, bf16[9,128,128]{2,1,0:T(8,128)(2,1)S(1)}, u32[]{:S(2)}, u32[]{:S(2)}) collective-permute-start(bf16[9,128,128]{2,1,0:T(8,128)(2,1)} %first_stage.1), channel_id=1, source_target_pairs={{0,2},{1,3},{2,4},{3,5},{4,6},{5,7},{6,0},{7,1},{8,10},{9,11},{10,... | collective-permute-start | bytes 884744 | tf_op jit(solution)/shard_map/ppermute | solution.py:39
  2.8 1.6 %copy-start = (bf16[1,1,63,128,128]{4,3,2,1,0:T(8,128)(2,1)S(1)}, bf16[1,1,63,128,128]{4,3,2,1,0:T(8,128)(2,1)}, u32[]{:S(2)}) copy-start(bf16[1,1,63,128,128]{4,3,2,1,0:T(8,128)(2,1)} %param.4) | copy-start | bytes 6193156
  4.4 42.2 %copy-start.1 = (bf16[1,1,63,128,128]{4,3,2,1,0:T(8,128)(2,1)S(1)}, bf16[1,1,63,128,128]{4,3,2,1,0:T(8,128)(2,1)}, u32[]{:S(2)}) copy-start(bf16[1,1,63,128,128]{4,3,2,1,0:T(8,128)(2,1)} %param.4) | copy-start | bytes 6193156
  7.3 2.1 %copy-start.11 = (bf16[9,128,128]{2,1,0:T(8,128)(2,1)}, bf16[9,128,128]{2,1,0:T(8,128)(2,1)S(1)}, u32[]{:S(2)}) copy-start(bf16[9,128,128]{2,1,0:T(8,128)(2,1)S(1)} %get-tuple-element.91) | copy-start | bytes 884740
  7.3 25.5 %copy-start.5 = (s32[63]{0:T(128)}, s32[63]{0:T(128)S(1)}, u32[]{:S(2)}) copy-start(s32[63]{0:T(128)S(1)} %get-tuple-element.75.pos) | copy-start | bytes 760
  7.3 21.6 %collective-permute-start = (bf16[10,128,128]{2,1,0:T(8,128)(2,1)}, bf16[10,128,128]{2,1,0:T(8,128)(2,1)}, u32[]{:S(2)}, u32[]{:S(2)}) collective-permute-start(bf16[10,128,128]{2,1,0:T(8,128)(2,1)} %get-tuple-element.59.self_ref), channel_id=1, source_target_pairs={{0,1},{1,2},{2,3},{3,4},{4,5},{5,6},{6,7},{7,0},{8,9},{9,10},{10,1... | collective-permute-start | bytes 983048 | tf_op jit(solution)/shard_map/ppermute | solution.py:39
  9.5 14.2 %collective-permute-start.2 = (bf16[9,128,128]{2,1,0:T(8,128)(2,1)S(1)}, bf16[9,128,128]{2,1,0:T(8,128)(2,1)S(1)}, u32[]{:S(2)}, u32[]{:S(2)}) collective-permute-start(bf16[9,128,128]{2,1,0:T(8,128)(2,1)S(1)} %get-tuple-element.61), channel_id=1, source_target_pairs={{0,6},{1,7},{2,0},{3,1},{4,2},{5,3},{6,4},{7,5},{8,14},{9,15},{10,... | collective-permute-start | bytes 884744 | tf_op jit(solution)/shard_map/ppermute | solution.py:39
  9.6 17.2 %collective-permute-start.1 = (bf16[9,128,128]{2,1,0:T(8,128)(2,1)}, bf16[9,128,128]{2,1,0:T(8,128)(2,1)S(1)}, u32[]{:S(2)}, u32[]{:S(2)}) collective-permute-start(bf16[9,128,128]{2,1,0:T(8,128)(2,1)} %get-tuple-element.60), channel_id=1, source_target_pairs={{0,7},{1,0},{2,1},{3,2},{4,3},{5,4},{6,5},{7,6},{8,15},{9,8},{10,9... | collective-permute-start | bytes 884744 | tf_op jit(solution)/shard_map/ppermute | solution.py:39
  10.7 25.1 %collective-permute-start.7 = (bf16[9,128,128]{2,1,0:T(8,128)(2,1)}, bf16[9,128,128]{2,1,0:T(8,128)(2,1)S(1)}, u32[]{:S(2)}, u32[]{:S(2)}) collective-permute-start(bf16[9,128,128]{2,1,0:T(8,128)(2,1)} %get-tuple-element.83), channel_id=1, source_target_pairs={{0,3},{1,4},{2,5},{3,6},{4,7},{5,0},{6,1},{7,2},{8,11},{9,12},{10,... | collective-permute-start | bytes 884744 | tf_op jit(solution)/shard_map/ppermute | solution.py:39
  13.3 30.7 %collective-permute-start.6 = (bf16[9,128,128]{2,1,0:T(8,128)(2,1)}, bf16[9,128,128]{2,1,0:T(8,128)(2,1)S(1)}, u32[]{:S(2)}, u32[]{:S(2)}) collective-permute-start(bf16[9,128,128]{2,1,0:T(8,128)(2,1)} %get-tuple-element.82), channel_id=1, source_target_pairs={{0,5},{1,6},{2,7},{3,0},{4,1},{5,2},{6,3},{7,4},{8,13},{9,14},{10,... | collective-permute-start | bytes 884744 | tf_op jit(solution)/shard_map/ppermute | solution.py:39
  23.7 5.3 %collective-permute-start.5 = (s32[63]{0:T(128)S(1)}, s32[63]{0:T(128)S(1)}, u32[]{:S(2)}, u32[]{:S(2)}) collective-permute-start(s32[63]{0:T(128)S(1)} %get-tuple-element.75.pos), channel_id=1, source_target_pairs={{0,24},{8,0},{16,8},{24,16},{1,25},{9,1},{17,9},{25,17},{2,26},{10... | collective-permute-start | bytes 764 | tf_op jit(solution)/shard_map/ppermute | solution.py:39
  26.8 3.1 %collective-permute-start.4 = (s32[24]{0:T(128)}, s32[24]{0:T(128)S(1)}, u32[]{:S(2)}, u32[]{:S(2)}) collective-permute-start(s32[24]{0:T(128)} %get-tuple-element.74), channel_id=1, source_target_pairs={{0,8},{8,16},{16,24},{24,0},{1,9},{9,17},{17,25},{25,1},{2,10},{10... | collective-permute-start | bytes 296 | tf_op jit(solution)/shard_map/ppermute | solution.py:39
  29.0 3.9 %copy-start.12 = (s32[63]{0:T(128)}, s32[63]{0:T(128)S(1)}, u32[]{:S(2)}) copy-start(s32[63]{0:T(128)S(1)} %collective-permute-done.5.pos_r) | copy-start | bytes 760
  44.0 15.9 %collective-permute-start.8 = (bf16[9,128,128]{2,1,0:T(8,128)(2,1)}, bf16[9,128,128]{2,1,0:T(8,128)(2,1)S(1)}, u32[]{:S(2)}, u32[]{:S(2)}) collective-permute-start(bf16[9,128,128]{2,1,0:T(8,128)(2,1)} %copy-done.11), channel_id=1, source_target_pairs={{0,4},{1,5},{2,6},{3,7},{4,0},{5,1},{6,2},{7,3},{8,12},{9,13},{10,... | collective-permute-start | bytes 884744 | tf_op jit(solution)/shard_map/ppermute | solution.py:39
  46.6 0.6 copy-start.6
  47.2 12.7 %copy-start.10 = (s32[25]{0:T(128)S(1)}, s32[25]{0:T(128)}, u32[]{:S(2)}) copy-start(s32[25]{0:T(128)} %asked.1.req) | copy-start | bytes 304
  48.9 12.9 %copy-start.3 = (s32[1,1,2,128,3]{3,2,4,1,0:T(2,128)S(1)}, s32[1,1,2,128,3]{3,2,4,1,0:T(2,128)}, u32[]{:S(2)}) copy-start(s32[1,1,2,128,3]{3,2,4,1,0:T(2,128)} %param.6) | copy-start | bytes 9220
  48.9 12.9 %copy-start.7 = (s32[63]{0:T(128)S(1)}, s32[63]{0:T(128)}, u32[]{:S(2)}) copy-start(s32[63]{0:T(128)} %copy-done.5) | copy-start | bytes 760
  48.9 12.9 %copy-start.8 = (s32[1,1,2]{2,1,0:T(1,128)S(1)}, s32[1,1,2]{2,1,0:T(1,128)}, u32[]{:S(2)}) copy-start(s32[1,1,2]{2,1,0:T(1,128)} %param.7) | copy-start | bytes 28
  48.9 26.4 %collective-permute-start.10 = (bf16[24,128,128]{2,1,0:T(8,128)(2,1)S(1)}, bf16[24,128,128]{2,1,0:T(8,128)(2,1)S(1)}, u32[]{:S(2)}, u32[]{:S(2)}) collective-permute-start(bf16[24,128,128]{2,1,0:T(8,128)(2,1)S(1)} %pick_right.1), channel_id=1, source_target_pairs={{0,24},{8,0},{16,8},{24,16},{1,25},{9,1},{17,9},{25,17},{2,26},{10... | collective-permute-start | bytes 2359304 | tf_op jit(solution)/shard_map/ppermute | solution.py:39
  61.2 14.1 %copy-start.4 = (s32[3,128]{1,0:T(4,128)S(1)}, s32[3,128]{1,0:T(4,128)}, u32[]{:S(2)}) copy-start(s32[3,128]{1,0:T(4,128)} %places.1.spots) | copy-start | bytes 4612
  61.2 14.1 %collective-permute-start.9 = (bf16[24,128,128]{2,1,0:T(8,128)(2,1)S(1)}, bf16[24,128,128]{2,1,0:T(8,128)(2,1)S(1)}, u32[]{:S(2)}, u32[]{:S(2)}) collective-permute-start(bf16[24,128,128]{2,1,0:T(8,128)(2,1)S(1)} %pick_left.1), channel_id=1, source_target_pairs={{0,7},{1,0},{2,1},{3,2},{4,3},{5,4},{6,5},{7,6},{8,15},{9,8},{10,9... | collective-permute-start | bytes 2359304 | tf_op jit(solution)/shard_map/ppermute | solution.py:39
  61.5 13.8 %collective-permute-start.11 = (bf16[9,128,128]{2,1,0:T(8,128)(2,1)S(1)}, bf16[9,128,128]{2,1,0:T(8,128)(2,1)S(1)}, u32[]{:S(2)}, u32[]{:S(2)}) collective-permute-start(bf16[9,128,128]{2,1,0:T(8,128)(2,1)S(1)} %collective-permute-done.8.rest_5_.rest_6_), channel_id=1, source_target_pairs={{0,24},{8,0},{16,8},{24,16},{1,25},{9,1},{17,9},{25,17},{2,26},{10... | collective-permute-start | bytes 884744 | tf_op jit(solution)/shard_map/ppermute | solution.py:39
